TPU v7x, 32 devices: a whole 2x2x4 slice. The times are simulated.
32 devices in a mesh: view: 16 (over z, x, core), row: 2 (over y).
Axes of the slice: x: 2, y: 2, z: 4, core: 2. Of those that a mesh axis runs over, the one named last changes fastest.
Arguments:
- layers: bfloat16 [3, 3, 96, 1024], P(None, None, 'row'), may hold values from 0.19921875 to 1
- target: bfloat16 [16, 96, 1024], P('view', 'row'), may hold values from 0.049804688 to 0.5
- shifts: int32 [16, 3, 2], P('view'), may hold values from -8 to 8, as said below
Outputs:
- updated: float32 [3, 3, 96, 1024], P(None, None, 'row')
Inputs may be any that keep to these rules, and one draw needn't show every extreme that they name: `shifts`: for every layer and each of the two components, one view has shift 8 and another view has shift -8.
All inputs are finite; a program needn't handle non-finite values.
Results may differ from a plain program's by a relative error of at most 0.0003.
Values may be sent and summed in bfloat16 or wider, within the bound.
A program may use at most 64 MiB of HBM per device.

v0:
```python
import jax
import jax.numpy as jnp
from jax import lax
from jax.sharding import PartitionSpec as P

HALO = 8


regular = 0.05


def padded(cells, sides, width):
    for axis, dim in sides:
        count = lax.axis_size(axis)
        ends = count - 1
        head = lax.slice_in_dim(cells, 0, width, axis=dim)
        tail = lax.slice_in_dim(cells, cells.shape[dim] - width, cells.shape[dim], axis=dim)
        cells = jnp.concatenate(
            [
                lax.ppermute(tail, axis, [(i, (i + 1) % count) for i in range(ends)]),
                cells,
                lax.ppermute(head, axis, [((i + 1) % count, i) for i in range(ends)]),
            ],
            axis=dim,
        )
    return cells


def product_except(pieces, skip):
    result = None
    for layer in range(len(pieces)):
        if layer != skip:
            result = pieces[layer] if result is None else result * pieces[layer]
    return result


def body(layers, target, shifts):
    frame_count, layer_count, row_count, col_count = layers.shape
    extended = padded(layers, (("row", 2),), HALO)
    widened = jnp.pad(extended, ((0, 0), (0, 0), (0, 0), (HALO, HALO)))
    zero = jnp.zeros((), jnp.int32)
    pieces = []
    for layer in range(layer_count):
        start_row = HALO + shifts[0, layer, 0]
        start_col = HALO + shifts[0, layer, 1]
        piece = lax.dynamic_slice(
            widened[:, layer], (zero, start_row, start_col), (frame_count, row_count, col_count)
        )
        pieces.append(piece.astype(jnp.float32))
    whole_product = pieces[0]
    for layer in range(1, layer_count):
        whole_product = whole_product * pieces[layer]
    shown = jnp.sum(whole_product, axis=0) / frame_count
    image = target[0].astype(jnp.float32)
    target_terms = jnp.stack(
        [image[None] * product_except(pieces, layer) for layer in range(layer_count)], axis=1
    )
    model_terms = jnp.stack(
        [shown[None] * product_except(pieces, layer) for layer in range(layer_count)], axis=1
    )
    stacked = jnp.stack([target_terms, model_terms])
    stacked = padded(stacked, (("row", 3),), HALO)
    stacked = jnp.pad(stacked, ((0, 0), (0, 0), (0, 0), (0, 0), (HALO, HALO)))
    backs = []
    for layer in range(layer_count):
        start_row = HALO - shifts[0, layer, 0]
        start_col = HALO - shifts[0, layer, 1]
        back = lax.dynamic_slice(
            stacked[:, :, layer],
            (zero, zero, start_row, start_col),
            (2, frame_count, row_count, col_count),
        )
        backs.append(back)
    upper = jnp.stack([back[0] for back in backs], axis=1)
    lower = jnp.stack([back[1] for back in backs], axis=1)
    upper_all, lower_all = lax.psum((upper, lower), "view")
    return layers.astype(jnp.float32) * (upper_all + regular) / (lower_all + regular)


def solution(mesh):
    placed = (P(None, None, "row", None), P("view", "row", None), P("view", None, None))
    return jax.shard_map(
        body, mesh=mesh, in_specs=placed, out_specs=P(None, None, "row", None), check_vma=False
    )
```

profile of v0, /device:TPU:1, one launch (start us, length us, event | category | flops | bytes accessed | tf_op | source)
XLA Modules:
  0.0 175.1 jit_solution(6861156110303629963)
XLA Ops:
  6.5 1.0 fusion.17
  7.5 4.0 %collective-permute-start = (bf16[3,3,8,1024]{3,2,0,1:T(8,128)(2,1)S(1)}, bf16[3,3,8,1024]{3,2,0,1:T(8,128)(2,1)S(1)}, u32[]{:S(2)}, u32[]{:S(2)}) collective-permute-start(bf16[3,3,8,1024]{3,2,0,1:T(8,128)(2,1)S(1)} %get-tuple-element.25), channel_id=1, source_target_pairs={{0,1},{2,3},{4,5},{6,7},{8,9},{10,11},{12,13},{14,15},{16,17},{18,... | collective-permute-start | bytes 442376 | tf_op jit(solution)/shard_map/ppermute | solution.py:20
  11.5 1.3 collective-permute-start.1
  12.8 1.6 fusion.18
  21.8 0.9 bitcast_convert_fusion
  22.7 1.8 %fusion.7 = bf16[3,3,64,1040]{3,2,0,1:T(8,128)(2,1)S(1)} fusion(bf16[3,3,8,1024]{3,2,0,1:T(8,128)(2,1)S(1)} %collective-permute-done.1, bf16[3,3,8,1024]{3,2,0,1:T(8,128)(2,1)S(1)} %collective-permute-done, bf16[3,3,48,1024]{3,2,1,0:T(8,128)(2,1)} %param.3), kind=kLoop, calls=%fused_computation.19 | loop fusion | flops 7188480 | bytes 2377728 | tf_op jit(solution)/shard_map/concatenate | solution.py:18
  24.6 0.1 fusion.16
  24.7 0.7 fusion.10
  25.4 0.6 fusion.9
  26.0 0.4 maximum_bitcast_fusion
  26.5 1.1 pad_maximum_fusion.3
  27.6 4.8 %collective-permute-start.2 = (f32[2,3,3,8,1024]{4,3,1,2,0:T(8,128)}, f32[2,3,3,8,1024]{4,3,1,2,0:T(8,128)}, u32[]{:S(2)}, u32[]{:S(2)}) collective-permute-start(f32[2,3,3,8,1024]{4,3,1,2,0:T(8,128)} %get-tuple-element.10), channel_id=1, source_target_pairs={{0,1},{2,3},{4,5},{6,7},{8,9},{10,11},{12,13},{14,15},{16,17},{18,... | collective-permute-start | bytes 1769480 | tf_op jit(solution)/shard_map/ppermute | solution.py:20
  32.4 1.3 collective-permute-start.3
  41.1 2.2 %collective-permute-done.2 = f32[2,3,3,8,1024]{4,3,1,2,0:T(8,128)} collective-permute-done((f32[2,3,3,8,1024]{4,3,1,2,0:T(8,128)}, f32[2,3,3,8,1024]{4,3,1,2,0:T(8,128)}, u32[]{:S(2)}, u32[]{:S(2)}) %collective-permute-start.2) | collective-permute-done | bytes 589856 | tf_op jit(solution)/shard_map/ppermute | solution.py:20
  43.2 4.7 %collective-permute-done.3 = f32[2,3,3,8,1024]{4,3,1,2,0:T(8,128)} collective-permute-done((f32[2,3,3,8,1024]{4,3,1,2,0:T(8,128)}, f32[2,3,3,8,1024]{4,3,1,2,0:T(8,128)}, u32[]{:S(2)}, u32[]{:S(2)}) %collective-permute-start.3) | collective-permute-done | bytes 589856 | tf_op jit(solution)/shard_map/ppermute | solution.py:22
  47.9 4.9 %select_maximum_fusion = f32[2,3,3,64,1040]{4,3,1,2,0:T(8,128)S(1)} fusion(f32[2,3,3,8,1024]{4,3,1,2,0:T(8,128)} %collective-permute-done.3, f32[2,3,3,8,1024]{4,3,1,2,0:T(8,128)} %collective-permute-done.2, f32[1,3,3,48,1024]{4,3,1,2,0:T(8,128)S(1)} %get-tuple-element.37, f32[1,3,3,48,1024]{4,3,1,2,0:T(8,128)S(1)} %get-tuple-element.36), kind=kLoop, calls=%fused_computation.2 | loop fusion | flops 11980800 | bytes 9510912 | tf_op jit(solution)/shard_map/concatenate | solution.py:18
  52.8 0.5 fusion.15
  53.2 0.4 dynamic-slice_bitcast_fusion.5
  53.6 0.4 dynamic-slice_bitcast_fusion.4
  54.0 0.4 dynamic-slice_bitcast_fusion.3
  54.4 1.4 pad_maximum_fusion
  55.8 1.4 pad_maximum_fusion.1
  57.2 107.1 %all-reduce.5.cloned.1.call-done = (f32[3,3,48,1024]{3,2,0,1:T(8,128)}, f32[3,3,48,1024]{3,2,1,0:T(8,128)}) async-done(((f32[3,3,48,1024]{3,2,0,1:T(8,128)}, f32[3,3,48,1024]{3,2,1,0:T(8,128)}), (f32[3,3,48,1024]{3,2,0,1:T(8,128)}, f32[3,3,48,1024]{3,2,1,0:T(8,128)})) %all-reduce.5.cloned.1.call-update) | async-done | bytes 3538960 | tf_op jit(solution)/shard_map/psum | solution.py:76
  164.4 3.8 %fusion.2 = f32[3,3,48,1024]{3,2,1,0:T(8,128)} fusion(f32[3,3,48,1024]{3,2,0,1:T(8,128)} %get-tuple-element.5, f32[3,3,48,1024]{3,2,1,0:T(8,128)} %get-tuple-element.6, bf16[3,3,48,1024]{3,2,1,0:T(8,128)(2,1)S(1)} %copy-done), kind=kLoop, calls=%fused_computation.14 | loop fusion | flops 2211840 | bytes 6193152 | tf_op jit(solution)/shard_map/div | solution.py:77
  (7 shorter events, 0.0 us)
Async XLA Ops:
  6.5 157.9 %all-reduce.5.cloned.1.call-start = ((), (), s32[]{:S(2)}) async-start(), calls=%async_computation | async-start | bytes 7077888 | tf_op jit(solution)/shard_map/psum | solution.py:76
  7.5 15.2 %collective-permute-start = (bf16[3,3,8,1024]{3,2,0,1:T(8,128)(2,1)S(1)}, bf16[3,3,8,1024]{3,2,0,1:T(8,128)(2,1)S(1)}, u32[]{:S(2)}, u32[]{:S(2)}) collective-permute-start(bf16[3,3,8,1024]{3,2,0,1:T(8,128)(2,1)S(1)} %get-tuple-element.25), channel_id=1, source_target_pairs={{0,1},{2,3},{4,5},{6,7},{8,9},{10,11},{12,13},{14,15},{16,17},{18,... | collective-permute-start | bytes 442376 | tf_op jit(solution)/shard_map/ppermute | solution.py:20
  11.5 11.2 %collective-permute-start.1 = (bf16[3,3,8,1024]{3,2,0,1:T(8,128)(2,1)S(1)}, bf16[3,3,8,1024]{3,2,0,1:T(8,128)(2,1)S(1)}, u32[]{:S(2)}, u32[]{:S(2)}) collective-permute-start(bf16[3,3,8,1024]{3,2,0,1:T(8,128)(2,1)S(1)} %get-tuple-element.26), channel_id=1, source_target_pairs={{1,0},{3,2},{5,4},{7,6},{9,8},{11,10},{13,12},{15,14},{17,16},{19,... | collective-permute-start | bytes 442376 | tf_op jit(solution)/shard_map/ppermute | solution.py:22
  27.6 15.7 %collective-permute-start.2 = (f32[2,3,3,8,1024]{4,3,1,2,0:T(8,128)}, f32[2,3,3,8,1024]{4,3,1,2,0:T(8,128)}, u32[]{:S(2)}, u32[]{:S(2)}) collective-permute-start(f32[2,3,3,8,1024]{4,3,1,2,0:T(8,128)} %get-tuple-element.10), channel_id=1, source_target_pairs={{0,1},{2,3},{4,5},{6,7},{8,9},{10,11},{12,13},{14,15},{16,17},{18,... | collective-permute-start | bytes 1769480 | tf_op jit(solution)/shard_map/ppermute | solution.py:20
  32.4 15.5 %collective-permute-start.3 = (f32[2,3,3,8,1024]{4,3,1,2,0:T(8,128)}, f32[2,3,3,8,1024]{4,3,1,2,0:T(8,128)}, u32[]{:S(2)}, u32[]{:S(2)}) collective-permute-start(f32[2,3,3,8,1024]{4,3,1,2,0:T(8,128)} %get-tuple-element.11), channel_id=1, source_target_pairs={{1,0},{3,2},{5,4},{7,6},{9,8},{11,10},{13,12},{15,14},{17,16},{19,... | collective-permute-start | bytes 1769480 | tf_op jit(solution)/shard_map/ppermute | solution.py:22
  57.2 107.2 %copy-start = (bf16[3,3,48,1024]{3,2,1,0:T(8,128)(2,1)S(1)}, bf16[3,3,48,1024]{3,2,1,0:T(8,128)(2,1)}, u32[]{:S(2)}) copy-start(bf16[3,3,48,1024]{3,2,1,0:T(8,128)(2,1)} %param.3) | copy-start | bytes 2654212
Sparse Core Ops, SparseCore 0:
  57.4 106.9 all-reduce.4
where the time goes:
time: 178 us; the launch traced here: 175 us
  waiting for transfers between devices  114 us (64%)
  between operations  28.3 us (16%)
  other arithmetic  17.1 us (10%)
  starting transfers between devices  11.4 us (6%)
  local copies, waits for them, and re-layouts  4.31 us (2%)
    psum x1, waiting for transfers between devices, body(): upper_all, lower_all = lax.psum((upper, lower), 'view')  107 us
    ppermute x2, starting transfers between devices, padded(): lax.ppermute(tail, axis, [(i, (i + 1) % count) for i in range(ends)])  8.81 us
    concatenate x2, other arithmetic, padded(): jnp.concatenate([lax.ppermute(tail, axis, [(i, (i + 1) % count) for i in...  6.66 us
    ppermute x2, waiting for transfers between devices, padded(): lax.ppermute(head, axis, [((i + 1) % count, i) for i in range(ends)])  4.66 us
    div x1, other arithmetic, body(): layers.astype(jnp.float32) * (upper_all + regular) / (lower_all + regular)  3.83 us
  transfers between devices with their start and end apart: 5, of which 3 were waited for; matrix products, arithmetic and copies ran while one was open for 1% of the time, Pallas kernels for 0%

commit v1 on v0

v1 whole, which is shorter than its diff:
```python
import functools
import math

import jax
import jax.numpy as jnp
from jax import lax
from jax.experimental import pallas as pl
from jax.experimental.pallas import tpu as pltpu
from jax.sharding import PartitionSpec as P

HALO = 8
LANES = 128
EDGE = 16
MARGIN = 32
REGULAR = 0.05
MESH = pl.DeviceIdType.MESH


def split_views(views):
    across = 1
    while (2 * across) ** 2 * 2 <= views:
        across *= 2
    return views // (2 * across), across


def code_range(views):
    low = math.log(REGULAR / (views + REGULAR))
    high = math.log((0.5 * views + REGULAR) / REGULAR)
    return 0.5 * (low + high), (high - low) / 65000.0


def kernel(
    views, rows_of, shifts_ref, layers_ref, target_ref, out_ref,
    send_win, recv_win, shift_out, shift_in, shift_smem, halo_out, halo_in,
    layer_win, target_win, others_win, shown_win, third_win, upper, lower, packed, slots,
    win_send, win_recv, up_send, up_recv, down_send, down_recv,
    shift_send, shift_recv, smem_sem, lh_send, lh_recv,
    col_send, x_send, core_send, slot_recv,
):
    frames, layer_count, rows, cols = layers_ref.shape
    strip = cols // views
    planes = frames * layer_count
    height = rows + 2 * EDGE
    inner = rows + 2 * HALO
    depth, across = split_views(views)
    groups = 2 if strip == 64 else 1
    short = rows // groups
    tiles = cols // LANES
    middle, step = code_range(views)

    me = lax.axis_index("view")
    row = lax.axis_index("row")
    above, below = row > 0, row < rows_of - 1

    barrier = pltpu.get_barrier_semaphore()

    def greet(j, carry):
        partner = lax.rem(me + j, views)

        @pl.when(j > 0)
        def _():
            pl.semaphore_signal(barrier, inc=1, device_id=(partner, row), device_id_type=MESH)

        @pl.when(above)
        def _():
            pl.semaphore_signal(barrier, inc=1, device_id=(partner, row - 1), device_id_type=MESH)

        @pl.when(below)
        def _():
            pl.semaphore_signal(barrier, inc=1, device_id=(partner, row + 1), device_id_type=MESH)

        return carry

    lax.fori_loop(0, views, greet, 0)

    lane = lax.broadcasted_iota(jnp.int32, (1, LANES), 1)

    def window(load, index):
        start = strip * index - MARGIN
        tile = (start + LANES) // LANES - 1
        offset = start - tile * LANES
        first = load(jnp.maximum(tile, 0))
        second = load(jnp.minimum(tile + 1, tiles - 1))
        turn = lax.rem(LANES - offset, LANES)
        first = pltpu.roll(first, turn, 1)
        second = pltpu.roll(second, turn, 1)
        both = jnp.where(lane < LANES - offset, first, second)
        col = start + lane
        return jnp.where((col >= 0) & (col < cols), both, 0.0)

    place = lax.broadcasted_iota(jnp.int32, (8, LANES), 1)
    block = jnp.zeros((8, LANES), jnp.int32)
    for k in range(layer_count):
        for axis in range(2):
            block = jnp.where(place == 2 * k + axis, shifts_ref[0, k, axis], block)
    shift_out[...] = block
    shift_in[me] = block

    def fill(c, carry):
        def load(tile):
            where = pl.ds(pl.multiple_of(tile * LANES, LANES), LANES)
            return target_ref[0, :, where].astype(jnp.float32)

        send_win[c] = window(load, c).astype(jnp.bfloat16)
        return carry

    lax.fori_loop(0, views, fill, 0)
    recv_win[me, EDGE : EDGE + rows, :] = send_win[me]

    for f in range(frames):
        for k in range(layer_count):
            def load(tile):
                where = pl.ds(pl.multiple_of(tile * LANES, LANES), LANES)
                return layers_ref[f, k, :, where].astype(jnp.float32)

            plane = window(load, me)
            at = f * layer_count + k
            layer_win[at, EDGE : EDGE + rows, :] = plane
            halo_out[0, at] = plane[:EDGE].astype(jnp.bfloat16)
            halo_out[1, at] = plane[rows - EDGE :].astype(jnp.bfloat16)

    def shift_copy(j):
        partner = lax.rem(me + j, views)
        return pltpu.make_async_remote_copy(
            src_ref=shift_out, dst_ref=shift_in.at[me], send_sem=shift_send.at[j],
            recv_sem=shift_recv.at[me], device_id=(partner, row), device_id_type=MESH,
        )

    def win_copy(j):
        partner = lax.rem(me + j, views)
        return pltpu.make_async_remote_copy(
            src_ref=send_win.at[partner], dst_ref=recv_win.at[me, pl.ds(EDGE, rows)],
            send_sem=win_send.at[j], recv_sem=win_recv.at[me],
            device_id=(partner, row), device_id_type=MESH,
        )

    def up_copy(j):
        partner = lax.rem(me + j, views)
        return pltpu.make_async_remote_copy(
            src_ref=send_win.at[partner, pl.ds(0, EDGE)],
            dst_ref=recv_win.at[me, pl.ds(EDGE + rows, EDGE)],
            send_sem=up_send.at[j], recv_sem=up_recv.at[me],
            device_id=(partner, row - 1), device_id_type=MESH,
        )

    def down_copy(j):
        partner = lax.rem(me + j, views)
        return pltpu.make_async_remote_copy(
            src_ref=send_win.at[partner, pl.ds(rows - EDGE, EDGE)],
            dst_ref=recv_win.at[me, pl.ds(0, EDGE)],
            send_sem=down_send.at[j], recv_sem=down_recv.at[me],
            device_id=(partner, row + 1), device_id_type=MESH,
        )

    def layer_copy(up):
        return pltpu.make_async_remote_copy(
            src_ref=halo_out.at[0 if up else 1], dst_ref=halo_in.at[1 if up else 0],
            send_sem=lh_send.at[0 if up else 1], recv_sem=lh_recv.at[1 if up else 0],
            device_id=(me, row - 1 if up else row + 1), device_id_type=MESH,
        )

    def arrived(dst, sem):
        return pltpu.make_async_remote_copy(
            src_ref=dst, dst_ref=dst, send_sem=sem, recv_sem=sem,
            device_id=(me, row), device_id_type=MESH,
        ).wait_recv()

    pl.semaphore_wait(
        barrier, views - 1 + views * (above.astype(jnp.int32) + below.astype(jnp.int32))
    )

    def send_shift(j, carry):
        shift_copy(j).start()
        return carry

    lax.fori_loop(1, views, send_shift, 0)

    @pl.when(above)
    def _():
        layer_copy(True).start()

    @pl.when(below)
    def _():
        layer_copy(False).start()

    def send_all(j, carry):
        @pl.when(j > 0)
        def _():
            win_copy(j).start()

        @pl.when(above)
        def _():
            up_copy(j).start()

        @pl.when(below)
        def _():
            down_copy(j).start()

        return carry

    lax.fori_loop(0, views, send_all, 0)

    @pl.when(jnp.logical_not(above))
    def _():
        recv_win[:, :EDGE, :] = jnp.zeros((views, EDGE, LANES), jnp.bfloat16)
        layer_win[:, :EDGE, :] = jnp.zeros((planes, EDGE, LANES), jnp.float32)

    @pl.when(jnp.logical_not(below))
    def _():
        recv_win[:, EDGE + rows :, :] = jnp.zeros((views, EDGE, LANES), jnp.bfloat16)
        layer_win[:, EDGE + rows :, :] = jnp.zeros((planes, EDGE, LANES), jnp.float32)

    at_row = rows * row - HALO + lax.broadcasted_iota(jnp.int32, (inner, LANES), 0)
    at_col = strip * me - MARGIN + lax.broadcasted_iota(jnp.int32, (inner, LANES), 1)
    inside = (at_row >= 0) & (at_row < rows * rows_of) & (at_col >= 0) & (at_col < cols)
    third_win[...] = jnp.where(inside, 1.0 / frames, 0.0)
    upper[...] = jnp.zeros_like(upper)
    lower[...] = jnp.zeros_like(lower)

    def wait_shift(j, carry):
        source = lax.rem(me + views - j, views)
        arrived(shift_in.at[source], shift_recv.at[source])
        return carry

    lax.fori_loop(1, views, wait_shift, 0)
    to_smem = pltpu.make_async_copy(shift_in, shift_smem, smem_sem)
    to_smem.start()

    @pl.when(above)
    def _():
        arrived(halo_in.at[0], lh_recv.at[0])
        layer_win[:, :EDGE, :] = halo_in[0].astype(jnp.float32)

    @pl.when(below)
    def _():
        arrived(halo_in.at[1], lh_recv.at[1])
        layer_win[:, EDGE + rows :, :] = halo_in[1].astype(jnp.float32)

    to_smem.wait()

    def one_view(j, carry):
        view = lax.rem(me + views - j, views)

        @pl.when(j > 0)
        def _():
            arrived(recv_win.at[view, pl.ds(EDGE, rows)], win_recv.at[view])

        @pl.when(above)
        def _():
            arrived(recv_win.at[view, pl.ds(0, EDGE)], down_recv.at[view])

        @pl.when(below)
        def _():
            arrived(recv_win.at[view, pl.ds(EDGE + rows, EDGE)], up_recv.at[view])

        target_win[...] = recv_win[view].astype(jnp.float32)
        row_shift = [shift_smem[view, 0, 2 * k] for k in range(layer_count)]
        col_shift = [shift_smem[view, 0, 2 * k + 1] for k in range(layer_count)]
        there = [lax.rem(LANES - c, LANES) for c in col_shift]
        back = [lax.rem(LANES + c, LANES) for c in col_shift]

        total = None
        for f in range(frames):
            seen = [
                pltpu.roll(
                    layer_win[f * layer_count + k, pl.ds(EDGE - HALO + row_shift[k], inner), :],
                    there[k], 1,
                )
                for k in range(layer_count)
            ]
            for k in range(layer_count):
                rest = None
                for i in range(layer_count):
                    if i != k:
                        rest = seen[i] if rest is None else rest * seen[i]
                others_win[f * layer_count + k] = rest
                if k == layer_count - 1:
                    whole = rest * seen[k]
                    total = whole if total is None else total + whole
        shown_win[...] = total * third_win[...]

        for k in range(layer_count):
            image = pltpu.roll(target_win[pl.ds(EDGE - row_shift[k], rows), :], back[k], 1)
            model = pltpu.roll(shown_win[pl.ds(HALO - row_shift[k], rows), :], back[k], 1)
            for f in range(frames):
                at = f * layer_count + k
                rest = pltpu.roll(
                    others_win[at, pl.ds(HALO - row_shift[k], rows), :], back[k], 1
                )
                upper[at] += image * rest
                lower[at] += model * rest
        return carry

    lax.fori_loop(0, views, one_view, 0)

    spare = packed.shape[0] - planes * short
    if spare:
        packed[planes * short :, :] = jnp.zeros((spare, LANES), jnp.float32)
    for at in range(planes):
        ratio = (upper[at] + REGULAR) / (lower[at] + REGULAR)
        value = (jnp.log(ratio) - middle) * (1.0 / step)
        merged = pltpu.roll(value[:short], LANES - MARGIN, 1)
        if groups == 2:
            merged = jnp.where(lane < strip, merged, pltpu.roll(value[short:], strip - MARGIN, 1))
        packed[at * short : (at + 1) * short, :] = merged
    slots[me] = jnp.round(packed[...]).astype(jnp.int32).astype(jnp.int16)

    core = lax.rem(me, 2)
    x = lax.rem(me // 2, across)
    z = me // (2 * across)

    def index(zz, xx, cc):
        return (zz * across + xx) * 2 + cc

    def slot_copy(slot, to, sem):
        return pltpu.make_async_remote_copy(
            src_ref=slots.at[slot], dst_ref=slots.at[slot], send_sem=sem,
            recv_sem=slot_recv.at[slot], device_id=(to, row), device_id_type=MESH,
        )

    def to_column(dz):
        return slot_copy(me, index(lax.rem(z + dz, depth), x, core), col_send.at[dz])

    def to_across(dz, dx):
        slot = index(lax.rem(z + depth - dz, depth), x, core)
        return slot_copy(slot, index(z, lax.rem(x + dx, across), core), x_send.at[dz, dx])

    def to_core(dz, dx):
        slot = index(lax.rem(z + depth - dz, depth), lax.rem(x + across - dx, across), core)
        return slot_copy(slot, index(z, x, 1 - core), core_send.at[dz, dx])

    for dz in range(1, depth):
        to_column(dz).start()
    for dx in range(1, across):
        to_across(0, dx).start()
    to_core(0, 0).start()
    for dz in range(1, depth):
        slot = index(lax.rem(z + depth - dz, depth), x, core)
        arrived(slots.at[slot], slot_recv.at[slot])
        for dx in range(1, across):
            to_across(dz, dx).start()
        to_core(dz, 0).start()
    for dz in range(depth):
        for dx in range(1, across):
            slot = index(lax.rem(z + depth - dz, depth), lax.rem(x + across - dx, across), core)
            arrived(slots.at[slot], slot_recv.at[slot])
            to_core(dz, dx).start()

    def wait_twin(n, carry):
        slot = 2 * n + 1 - core
        arrived(slots.at[slot], slot_recv.at[slot])
        return carry

    lax.fori_loop(0, views // 2, wait_twin, 0)

    per_tile = LANES // strip

    def unpack(tile, carry):
        where = pl.ds(pl.multiple_of(tile * LANES, LANES), LANES)
        parts = []
        for i in range(per_tile):
            code = slots[tile * per_tile + i].astype(jnp.int32).astype(jnp.float32)
            parts.append(jnp.exp(code * step + middle))
        for f in range(frames):
            for k in range(layer_count):
                at = f * layer_count + k
                for g in range(groups):
                    ratio = None
                    for i in range(per_tile):
                        part = parts[i][at * short : (at + 1) * short]
                        turn = (strip * (i - g)) % LANES
                        if turn:
                            part = pltpu.roll(part, turn, 1)
                        ratio = part if ratio is None else jnp.where(lane < strip * i, ratio, part)
                    span = slice(g * short, (g + 1) * short)
                    out_ref[f, k, span, where] = (
                        layers_ref[f, k, span, where].astype(jnp.float32) * ratio
                    )
        return carry

    lax.fori_loop(0, tiles, unpack, 0)

    for dz in range(1, depth):
        to_column(dz).wait_send()
    for dz in range(depth):
        for dx in range(across):
            if dx:
                to_across(dz, dx).wait_send()
            to_core(dz, dx).wait_send()

    @pl.when(above)
    def _():
        layer_copy(True).wait_send()

    @pl.when(below)
    def _():
        layer_copy(False).wait_send()

    def finish(j, carry):
        @pl.when(j > 0)
        def _():
            shift_copy(j).wait_send()
            win_copy(j).wait_send()

        @pl.when(above)
        def _():
            up_copy(j).wait_send()

        @pl.when(below)
        def _():
            down_copy(j).wait_send()

        return carry

    lax.fori_loop(0, views, finish, 0)


def body(views, rows_of, layers, target, shifts):
    frames, layer_count, rows, cols = layers.shape
    planes = frames * layer_count
    strip = cols // views
    groups = 2 if strip == 64 else 1
    depth, across = split_views(views)
    packed_rows = -(-planes * (rows // groups) // 16) * 16
    height, inner = rows + 2 * EDGE, rows + 2 * HALO
    dma = pltpu.SemaphoreType.DMA
    f32, bf16 = jnp.float32, jnp.bfloat16
    return pl.pallas_call(
        functools.partial(kernel, views, rows_of),
        out_shape=jax.ShapeDtypeStruct(layers.shape, f32),
        in_specs=[
            pl.BlockSpec(memory_space=pltpu.SMEM),
            pl.BlockSpec(memory_space=pltpu.VMEM),
            pl.BlockSpec(memory_space=pltpu.VMEM),
        ],
        out_specs=pl.BlockSpec(memory_space=pltpu.VMEM),
        scratch_shapes=[
            pltpu.VMEM((views, rows, LANES), bf16),
            pltpu.VMEM((views, height, LANES), bf16),
            pltpu.VMEM((8, LANES), jnp.int32),
            pltpu.VMEM((views, 8, LANES), jnp.int32),
            pltpu.SMEM((views, 8, LANES), jnp.int32),
            pltpu.VMEM((2, planes, EDGE, LANES), bf16),
            pltpu.VMEM((2, planes, EDGE, LANES), bf16),
            pltpu.VMEM((planes, height, LANES), f32),
            pltpu.VMEM((height, LANES), f32),
            pltpu.VMEM((planes, inner, LANES), f32),
            pltpu.VMEM((inner, LANES), f32),
            pltpu.VMEM((inner, LANES), f32),
            pltpu.VMEM((planes, rows, LANES), f32),
            pltpu.VMEM((planes, rows, LANES), f32),
            pltpu.VMEM((packed_rows, LANES), f32),
            pltpu.VMEM((views, packed_rows, LANES), jnp.int16),
            dma((views,)), dma((views,)), dma((views,)), dma((views,)), dma((views,)), dma((views,)),
            dma((views,)), dma((views,)), dma, dma((2,)), dma((2,)),
            dma((depth,)), dma((depth, across)), dma((depth, across)), dma((views,)),
        ],
        compiler_params=pltpu.CompilerParams(
            collective_id=0, has_side_effects=True, vmem_limit_bytes=40 * 1024 * 1024
        ),
        name="light_field_update",
    )(shifts, layers, target)


def solution(mesh):
    placed = (P(None, None, "row", None), P("view", "row", None), P("view", None, None))
    return jax.shard_map(
        functools.partial(body, mesh.shape["view"], mesh.shape["row"]),
        mesh=mesh, in_specs=placed, out_specs=P(None, None, "row", None), check_vma=False,
    )
```

time: 178 us -> 37.1 us (0.21); the launches traced: 175 us -> 36.6 us
  waiting for transfers between devices: 114 us -> 0 us
  Pallas kernels: 0 us -> 32.6 us
  between operations: 28.3 us -> 0.01 us
  other arithmetic: 17.1 us -> 0 us
  starting transfers between devices: 11.4 us -> 0 us
    psum x1 -> x0, waiting for transfers between devices: 107 us -> none  [body(): upper_all, lower_all = lax.psum((upper, lower), 'view')]
    pallas_call x0 -> x1, Pallas kernels: none -> 32.6 us  [body(): pl.pallas_call(functools.partial(kernel, views, rows_of), out_shape=jax.S...]
    ppermute x4 -> x0, starting transfers between devices: 11.4 us -> none  [the longest x2 8.81 us: padded(): lax.ppermute(tail, axis, [(i, (i + 1) % count) for i in range(ends)])]
    ppermute x4 -> x0, waiting for transfers between devices: 6.83 us -> none  [the longest x2 4.66 us: padded(): lax.ppermute(head, axis, [((i + 1) % count, i) for i in range(ends)])]
    concatenate x2 -> x0, other arithmetic: 6.66 us -> none  [padded(): jnp.concatenate([lax.ppermute(tail, axis, [(i, (i + 1) % count) for i in...]
    unnamed x2 -> x6, local copies, waits for them, and re-layouts: 0.01 us -> 4.03 us
    div x2 -> x0, other arithmetic: 3.85 us -> none  [the longest x1 3.83 us: body(): layers.astype(jnp.float32) * (upper_all + regular) / (lower_all + regular)]
    another operation x3 -> x0, other arithmetic: 3.25 us -> none  [the longest x1 1.42 us: body(): upper = jnp.stack([back[0] for back in backs], axis=1)]
  transfers between devices with their start and end apart: 5 -> 0, of which waited for: 3 -> 0; matrix products, arithmetic and copies ran while one was open for 1% -> 0% of each run, Pallas kernels for 0% -> 0%
where the time goes in v1:
time: 37.1 us; the launch traced here: 36.6 us
  Pallas kernels  32.6 us (88%)
  local copies, waits for them, and re-layouts  4.03 us (11%)
    pallas_call x1, Pallas kernels, body(): pl.pallas_call(functools.partial(kernel, views, rows_of), out_shape=jax.S...  32.6 us
    unnamed x6, local copies, waits for them, and re-layouts  4.03 us

profile of v1, /device:TPU:1, one launch (start us, length us, event | category | flops | bytes accessed | tf_op | source)
XLA Modules:
  0.0 36.6 jit_solution(7880902687462376189)
XLA Ops:
  0.0 0.8 %copy.4.shifts_ref = s32[1,3,2]{2,1,0:T(4,128)S(1)} copy(s32[1,3,2]{1,2,0:T(2,128)} %param.5) | data formatting | bytes 48 | tf_op args[2]
  0.8 0.0 copy-start
  0.8 1.2 %copy-done = bf16[3,3,48,1024]{3,2,1,0:T(8,128)(2,1)S(1)} copy-done((bf16[3,3,48,1024]{3,2,1,0:T(8,128)(2,1)S(1)}, bf16[3,3,48,1024]{3,2,1,0:T(8,128)(2,1)}, u32[]{:S(2)}) %copy-start) | copy-done | bytes 884760
  1.9 0.0 copy-start.1
  1.9 0.9 %copy-done.1 = bf16[1,48,1024]{2,1,0:T(8,128)(2,1)S(1)} copy-done((bf16[1,48,1024]{2,1,0:T(8,128)(2,1)S(1)}, bf16[1,48,1024]{2,1,0:T(8,128)(2,1)}, u32[]{:S(2)}) %copy-start.1) | copy-done | bytes 98328
  2.8 32.6 %light_field_update.1 = f32[3,3,48,1024]{3,2,1,0:T(8,128)S(1)} custom-call(s32[1,3,2]{2,1,0:T(4,128)S(1)} %copy.4.shifts_ref, bf16[3,3,48,1024]{3,2,1,0:T(8,128)(2,1)S(1)} %copy-done, bf16[1,48,1024]{2,1,0:T(8,128)(2,1)S(1)} %copy-done.1), custom_call_target="tpu_custom_call" | custom-call | tf_op jit(solution)/shard_map/light_field_update/pallas_call | solution.py:428
  35.4 1.2 %copy.6 = f32[3,3,48,1024]{3,2,1,0:T(8,128)} copy(f32[3,3,48,1024]{3,2,1,0:T(8,128)S(1)} %light_field_update.1) | data formatting | bytes 3538944
Async XLA Ops:
  0.8 1.2 %copy-start = (bf16[3,3,48,1024]{3,2,1,0:T(8,128)(2,1)S(1)}, bf16[3,3,48,1024]{3,2,1,0:T(8,128)(2,1)}, u32[]{:S(2)}) copy-start(bf16[3,3,48,1024]{3,2,1,0:T(8,128)(2,1)} %layers_ref.1) | copy-start | bytes 2654212
  1.9 0.9 %copy-start.1 = (bf16[1,48,1024]{2,1,0:T(8,128)(2,1)S(1)}, bf16[1,48,1024]{2,1,0:T(8,128)(2,1)}, u32[]{:S(2)}) copy-start(bf16[1,48,1024]{2,1,0:T(8,128)(2,1)} %target_ref.1) | copy-start | bytes 294916

commit v2 on v1

--- a/solution.py
+++ b/solution.py
@@ -30,13 +30,21 @@
 
 
 def kernel(
-    views, rows_of, shifts_ref, layers_ref, target_ref, out_ref,
+    views, rows_of, shifts_hbm, layers_hbm, target_hbm, out_ref,
+    shifts_ref, layers_ref, target_ref, fetch_sem,
     send_win, recv_win, shift_out, shift_in, shift_smem, halo_out, halo_in,
     layer_win, target_win, others_win, shown_win, third_win, upper, lower, packed, slots,
     win_send, win_recv, up_send, up_recv, down_send, down_recv,
     shift_send, shift_recv, smem_sem, lh_send, lh_recv,
     col_send, x_send, core_send, slot_recv,
 ):
+    fetch_shifts = pltpu.make_async_copy(shifts_hbm, shifts_ref, fetch_sem.at[0])
+    fetch_target = pltpu.make_async_copy(target_hbm, target_ref, fetch_sem.at[1])
+    fetch_layers = pltpu.make_async_copy(layers_hbm, layers_ref, fetch_sem.at[2])
+    fetch_shifts.start()
+    fetch_target.start()
+    fetch_layers.start()
+
     frames, layer_count, rows, cols = layers_ref.shape
     strip = cols // views
     planes = frames * layer_count
@@ -88,13 +96,16 @@
         col = start + lane
         return jnp.where((col >= 0) & (col < cols), both, 0.0)
 
+    fetch_shifts.wait()
     place = lax.broadcasted_iota(jnp.int32, (8, LANES), 1)
     block = jnp.zeros((8, LANES), jnp.int32)
     for k in range(layer_count):
         for axis in range(2):
-            block = jnp.where(place == 2 * k + axis, shifts_ref[0, k, axis], block)
+            block = jnp.where(place == 2 * k + axis, shifts_ref[0, axis, k], block)
     shift_out[...] = block
     shift_in[me] = block
+
+    fetch_target.wait()
 
     def fill(c, carry):
         def load(tile):
@@ -107,6 +118,7 @@
     lax.fori_loop(0, views, fill, 0)
     recv_win[me, EDGE : EDGE + rows, :] = send_win[me]
 
+    fetch_layers.wait()
     for f in range(frames):
         for k in range(layer_count):
             def load(tile):
@@ -318,44 +330,77 @@
             recv_sem=slot_recv.at[slot], device_id=(to, row), device_id_type=MESH,
         )
 
-    def to_column(dz):
-        return slot_copy(me, index(lax.rem(z + dz, depth), x, core), col_send.at[dz])
-
-    def to_across(dz, dx):
-        slot = index(lax.rem(z + depth - dz, depth), x, core)
-        return slot_copy(slot, index(z, lax.rem(x + dx, across), core), x_send.at[dz, dx])
-
-    def to_core(dz, dx):
-        slot = index(lax.rem(z + depth - dz, depth), lax.rem(x + across - dx, across), core)
-        return slot_copy(slot, index(z, x, 1 - core), core_send.at[dz, dx])
-
-    for dz in range(1, depth):
-        to_column(dz).start()
-    for dx in range(1, across):
-        to_across(0, dx).start()
-    to_core(0, 0).start()
-    for dz in range(1, depth):
-        slot = index(lax.rem(z + depth - dz, depth), x, core)
-        arrived(slots.at[slot], slot_recv.at[slot])
+    def along(d):
+        return index(z + d, x, core)
+
+    def to_next(d, way):
+        return slot_copy(along(d), index(z + way, x, core), col_send.at[depth + d, (way + 1) // 2])
+
+    def to_across(d, dx):
+        return slot_copy(
+            along(d), index(z, lax.rem(x + dx, across), core), x_send.at[depth + d, dx]
+        )
+
+    def to_core(d, dx):
+        slot = index(z + d, lax.rem(x + across - dx, across), core)
+        return slot_copy(slot, index(z, x, 1 - core), core_send.at[depth + d, dx])
+
+    def exists(d):
+        return (z + d >= 0) & (z + d < depth)
+
+    def outward(d):
+        return [d // abs(d) * -1] if d else [-1, 1]
+
+    def visit(d, act):
+        if d:
+            pl.when(exists(d))(act)
+        else:
+            act()
+
+    def both_ways(d):
+        return (-d, d) if d else (0,)
+
+    def each_copy(d, act):
+        for way in outward(d):
+            pl.when(exists(way))(lambda: act(to_next(d, way)))
         for dx in range(1, across):
-            to_across(dz, dx).start()
-        to_core(dz, 0).start()
-    for dz in range(depth):
-        for dx in range(1, across):
-            slot = index(lax.rem(z + depth - dz, depth), lax.rem(x + across - dx, across), core)
-            arrived(slots.at[slot], slot_recv.at[slot])
-            to_core(dz, dx).start()
-
-    def wait_twin(n, carry):
-        slot = 2 * n + 1 - core
-        arrived(slots.at[slot], slot_recv.at[slot])
-        return carry
-
-    lax.fori_loop(0, views // 2, wait_twin, 0)
+            act(to_across(d, dx))
+        act(to_core(d, 0))
+
+    def column_step(d):
+        def act():
+            if d:
+                slot = along(d)
+                arrived(slots.at[slot], slot_recv.at[slot])
+            each_copy(d, lambda copy: copy.start())
+
+        visit(d, act)
+
+    def across_step(d):
+        def act():
+            for dx in range(1, across):
+                slot = index(z + d, lax.rem(x + across - dx, across), core)
+                arrived(slots.at[slot], slot_recv.at[slot])
+                to_core(d, dx).start()
+
+        visit(d, act)
+
+    column_step(0)
+    for distance in range(1, depth):
+        for d in both_ways(distance):
+            column_step(d)
+        for d in both_ways(distance - 1):
+            across_step(d)
 
     per_tile = LANES // strip
 
-    def unpack(tile, carry):
+    def unpack(tile):
+        for i in range(per_tile):
+            @pl.when(lax.rem(tile * per_tile + i, 2) != core)
+            def _():
+                slot = tile * per_tile + i
+                arrived(slots.at[slot], slot_recv.at[slot])
+
         where = pl.ds(pl.multiple_of(tile * LANES, LANES), LANES)
         parts = []
         for i in range(per_tile):
@@ -376,17 +421,40 @@
                     out_ref[f, k, span, where] = (
                         layers_ref[f, k, span, where].astype(jnp.float32) * ratio
                     )
-        return carry
-
-    lax.fori_loop(0, tiles, unpack, 0)
-
-    for dz in range(1, depth):
-        to_column(dz).wait_send()
-    for dz in range(depth):
-        for dx in range(across):
-            if dx:
-                to_across(dz, dx).wait_send()
-            to_core(dz, dx).wait_send()
+
+    early = strip == 64
+
+    def unpack_column(n, carry):
+        unpack(n * across + x)
+        return carry
+
+    if early:
+        lax.fori_loop(0, depth, unpack_column, 0)
+    for d in both_ways(depth - 1):
+        across_step(d)
+
+    def unpack_rest(n, carry):
+        zz, dx = n // (across - 1), lax.rem(n, across - 1) + 1
+        unpack(zz * across + lax.rem(x + dx, across))
+        return carry
+
+    def unpack_any(n, carry):
+        unpack(n)
+        return carry
+
+    if early:
+        lax.fori_loop(0, depth * (across - 1), unpack_rest, 0)
+    else:
+        lax.fori_loop(0, tiles, unpack_any, 0)
+
+    for distance in range(depth):
+        for d in both_ways(distance):
+            def act():
+                each_copy(d, lambda copy: copy.wait_send())
+                for dx in range(1, across):
+                    to_core(d, dx).wait_send()
+
+            visit(d, act)
 
     @pl.when(above)
     def _():
@@ -429,12 +497,16 @@
         functools.partial(kernel, views, rows_of),
         out_shape=jax.ShapeDtypeStruct(layers.shape, f32),
         in_specs=[
-            pl.BlockSpec(memory_space=pltpu.SMEM),
-            pl.BlockSpec(memory_space=pltpu.VMEM),
-            pl.BlockSpec(memory_space=pltpu.VMEM),
+            pl.BlockSpec(memory_space=pl.ANY),
+            pl.BlockSpec(memory_space=pl.ANY),
+            pl.BlockSpec(memory_space=pl.ANY),
         ],
         out_specs=pl.BlockSpec(memory_space=pltpu.VMEM),
         scratch_shapes=[
+            pltpu.SMEM((1, 2, layer_count), jnp.int32),
+            pltpu.VMEM(layers.shape, bf16),
+            pltpu.VMEM(target.shape, bf16),
+            dma((3,)),
             pltpu.VMEM((views, rows, LANES), bf16),
             pltpu.VMEM((views, height, LANES), bf16),
             pltpu.VMEM((8, LANES), jnp.int32),
@@ -453,13 +525,13 @@
             pltpu.VMEM((views, packed_rows, LANES), jnp.int16),
             dma((views,)), dma((views,)), dma((views,)), dma((views,)), dma((views,)), dma((views,)),
             dma((views,)), dma((views,)), dma, dma((2,)), dma((2,)),
-            dma((depth,)), dma((depth, across)), dma((depth, across)), dma((views,)),
+            dma((2 * depth, 2)), dma((2 * depth, across)), dma((2 * depth, across)), dma((views,)),
         ],
         compiler_params=pltpu.CompilerParams(
             collective_id=0, has_side_effects=True, vmem_limit_bytes=40 * 1024 * 1024
         ),
         name="light_field_update",
-    )(shifts, layers, target)
+    )(jnp.swapaxes(shifts, 1, 2), layers, target)
 
 
 def solution(mesh):

time: 37.1 us -> 40.1 us (1.081)
  Pallas kernels: 32.6 us -> 36 us
    pallas_call x1, Pallas kernels: 32.6 us -> 36 us  [body(): pl.pallas_call(functools.partial(kernel, views, rows_of), out_shape=jax.S...]
    unnamed x6 -> x7, local copies, waits for them, and re-layouts: 4.03 us -> 3.95 us
where the time goes in v2:
time: 40.1 us; the launch traced here: 39.9 us
  Pallas kernels  36 us (90%)
  local copies, waits for them, and re-layouts  3.95 us (10%)
    pallas_call x1, Pallas kernels, body(): pl.pallas_call(functools.partial(kernel, views, rows_of), out_shape=jax.S...  36 us
    unnamed x7, local copies, waits for them, and re-layouts  3.95 us

profile of v2, /device:TPU:1, one launch (start us, length us, event | category | flops | bytes accessed | tf_op | source)
XLA Modules:
  0.0 39.9 jit_solution(16389162432629683893)
XLA Ops:
  0.0 0.0 copy-start
  0.0 1.2 %copy-done = bf16[3,3,48,1024]{3,2,1,0:T(8,128)(2,1)S(1)} copy-done((bf16[3,3,48,1024]{3,2,1,0:T(8,128)(2,1)S(1)}, bf16[3,3,48,1024]{3,2,1,0:T(8,128)(2,1)}, u32[]{:S(2)}) %copy-start) | copy-done | bytes 884760
  1.2 0.0 copy-start.1
  1.2 0.9 %copy-done.1 = bf16[1,48,1024]{2,1,0:T(8,128)(2,1)S(1)} copy-done((bf16[1,48,1024]{2,1,0:T(8,128)(2,1)S(1)}, bf16[1,48,1024]{2,1,0:T(8,128)(2,1)}, u32[]{:S(2)}) %copy-start.1) | copy-done | bytes 98328
  2.1 0.0 copy-start.2
  2.1 0.7 %copy-done.2 = s32[1,3,2]{1,2,0:T(2,128)S(1)} copy-done((s32[1,3,2]{1,2,0:T(2,128)S(1)}, s32[1,3,2]{1,2,0:T(2,128)}, u32[]{:S(2)}) %copy-start.2) | copy-done | bytes 48
  2.7 36.0 %light_field_update.1 = f32[3,3,48,1024]{3,2,1,0:T(8,128)S(1)} custom-call(s32[1,2,3]{2,1,0:T(2,128)S(1)} %bitcast.1, bf16[3,3,48,1024]{3,2,1,0:T(8,128)(2,1)S(1)} %copy-done, bf16[1,48,1024]{2,1,0:T(8,128)(2,1)S(1)} %copy-done.1), custom_call_target="tpu_custom_call" | custom-call | tf_op jit(solution)/shard_map/light_field_update/pallas_call | solution.py:496
  38.7 1.2 %copy.5 = f32[3,3,48,1024]{3,2,1,0:T(8,128)} copy(f32[3,3,48,1024]{3,2,1,0:T(8,128)S(1)} %light_field_update.1) | data formatting | bytes 3538944
Async XLA Ops:
  0.0 1.2 %copy-start = (bf16[3,3,48,1024]{3,2,1,0:T(8,128)(2,1)S(1)}, bf16[3,3,48,1024]{3,2,1,0:T(8,128)(2,1)}, u32[]{:S(2)}) copy-start(bf16[3,3,48,1024]{3,2,1,0:T(8,128)(2,1)} %layers_hbm.1) | copy-start | bytes 2654212
  1.2 0.9 %copy-start.1 = (bf16[1,48,1024]{2,1,0:T(8,128)(2,1)S(1)}, bf16[1,48,1024]{2,1,0:T(8,128)(2,1)}, u32[]{:S(2)}) copy-start(bf16[1,48,1024]{2,1,0:T(8,128)(2,1)} %target_hbm.1) | copy-start | bytes 294916
  2.1 0.7 %copy-start.2 = (s32[1,3,2]{1,2,0:T(2,128)S(1)}, s32[1,3,2]{1,2,0:T(2,128)}, u32[]{:S(2)}) copy-start(s32[1,3,2]{1,2,0:T(2,128)} %param.5) | copy-start | bytes 76

commit v3 on v2

--- a/solution.py
+++ b/solution.py
@@ -30,8 +30,8 @@
 
 
 def kernel(
-    views, rows_of, shifts_hbm, layers_hbm, target_hbm, out_ref,
-    shifts_ref, layers_ref, target_ref, fetch_sem,
+    views, rows_of, shifts_hbm, layers_hbm, target_hbm, out_hbm,
+    shifts_ref, layers_ref, target_ref, out_ref, fetch_sem, store_sem,
     send_win, recv_win, shift_out, shift_in, shift_smem, halo_out, halo_in,
     layer_win, target_win, others_win, shown_win, third_win, upper, lower, packed, slots,
     win_send, win_recv, up_send, up_recv, down_send, down_recv,
@@ -115,7 +115,7 @@
         send_win[c] = window(load, c).astype(jnp.bfloat16)
         return carry
 
-    lax.fori_loop(0, views, fill, 0)
+    lax.fori_loop(0, views, fill, 0, unroll=4)
     recv_win[me, EDGE : EDGE + rows, :] = send_win[me]
 
     fetch_layers.wait()
@@ -333,8 +333,8 @@
     def along(d):
         return index(z + d, x, core)
 
-    def to_next(d, way):
-        return slot_copy(along(d), index(z + way, x, core), col_send.at[depth + d, (way + 1) // 2])
+    def to_column(d):
+        return slot_copy(me, index(z + d, x, core), col_send.at[depth + d])
 
     def to_across(d, dx):
         return slot_copy(
@@ -347,9 +347,6 @@
 
     def exists(d):
         return (z + d >= 0) & (z + d < depth)
-
-    def outward(d):
-        return [d // abs(d) * -1] if d else [-1, 1]
 
     def visit(d, act):
         if d:
@@ -361,18 +358,22 @@
         return (-d, d) if d else (0,)
 
     def each_copy(d, act):
-        for way in outward(d):
-            pl.when(exists(way))(lambda: act(to_next(d, way)))
+        if d:
+            act(to_column(d))
         for dx in range(1, across):
             act(to_across(d, dx))
         act(to_core(d, 0))
 
+    def spread(d):
+        for dx in range(1, across):
+            to_across(d, dx).start()
+        to_core(d, 0).start()
+
     def column_step(d):
         def act():
-            if d:
-                slot = along(d)
-                arrived(slots.at[slot], slot_recv.at[slot])
-            each_copy(d, lambda copy: copy.start())
+            slot = along(d)
+            arrived(slots.at[slot], slot_recv.at[slot])
+            spread(d)
 
         visit(d, act)
 
@@ -385,7 +386,13 @@
 
         visit(d, act)
 
-    column_step(0)
+    for distance in range(depth - 1, 0, -1):
+        for d in both_ways(distance):
+            def act():
+                to_column(d).start()
+
+            visit(d, act)
+    spread(0)
     for distance in range(1, depth):
         for d in both_ways(distance):
             column_step(d)
@@ -393,6 +400,12 @@
             across_step(d)
 
     per_tile = LANES // strip
+
+    def store_tile(tile):
+        where = pl.ds(pl.multiple_of(tile * LANES, LANES), LANES)
+        return pltpu.make_async_copy(
+            out_ref.at[:, :, :, where], out_hbm.at[:, :, :, where], store_sem.at[tile]
+        )
 
     def unpack(tile):
         for i in range(per_tile):
@@ -421,6 +434,7 @@
                     out_ref[f, k, span, where] = (
                         layers_ref[f, k, span, where].astype(jnp.float32) * ratio
                     )
+        store_tile(tile).start()
 
     early = strip == 64
 
@@ -481,6 +495,12 @@
         return carry
 
     lax.fori_loop(0, views, finish, 0)
+
+    def wait_store(tile, carry):
+        store_tile(tile).wait()
+        return carry
+
+    lax.fori_loop(0, tiles, wait_store, 0)
 
 
 def body(views, rows_of, layers, target, shifts):
@@ -497,16 +517,18 @@
         functools.partial(kernel, views, rows_of),
         out_shape=jax.ShapeDtypeStruct(layers.shape, f32),
         in_specs=[
-            pl.BlockSpec(memory_space=pl.ANY),
-            pl.BlockSpec(memory_space=pl.ANY),
-            pl.BlockSpec(memory_space=pl.ANY),
+            pl.BlockSpec(memory_space=pltpu.HBM),
+            pl.BlockSpec(memory_space=pltpu.HBM),
+            pl.BlockSpec(memory_space=pltpu.HBM),
         ],
-        out_specs=pl.BlockSpec(memory_space=pltpu.VMEM),
+        out_specs=pl.BlockSpec(memory_space=pltpu.HBM),
         scratch_shapes=[
             pltpu.SMEM((1, 2, layer_count), jnp.int32),
             pltpu.VMEM(layers.shape, bf16),
             pltpu.VMEM(target.shape, bf16),
+            pltpu.VMEM(layers.shape, f32),
             dma((3,)),
+            dma((cols // LANES,)),
             pltpu.VMEM((views, rows, LANES), bf16),
             pltpu.VMEM((views, height, LANES), bf16),
             pltpu.VMEM((8, LANES), jnp.int32),
@@ -525,10 +547,10 @@
             pltpu.VMEM((views, packed_rows, LANES), jnp.int16),
             dma((views,)), dma((views,)), dma((views,)), dma((views,)), dma((views,)), dma((views,)),
             dma((views,)), dma((views,)), dma, dma((2,)), dma((2,)),
-            dma((2 * depth, 2)), dma((2 * depth, across)), dma((2 * depth, across)), dma((views,)),
+            dma((2 * depth,)), dma((2 * depth, across)), dma((2 * depth, across)), dma((views,)),
         ],
         compiler_params=pltpu.CompilerParams(
-            collective_id=0, has_side_effects=True, vmem_limit_bytes=40 * 1024 * 1024
+            collective_id=0, has_side_effects=True, vmem_limit_bytes=62 * 1024 * 1024
         ),
         name="light_field_update",
     )(jnp.swapaxes(shifts, 1, 2), layers, target)

time: 40.1 us -> 37.1 us (0.925)
  Pallas kernels: 36 us -> 33.9 us
  local copies, waits for them, and re-layouts: 3.95 us -> 2.89 us
    pallas_call x1, Pallas kernels: 36 us -> 33.9 us  [body(): pl.pallas_call(functools.partial(kernel, views, rows_of), out_shape=jax.S...]
    unnamed x7 -> x1, local copies, waits for them, and re-layouts: 3.95 us -> 2.89 us
where the time goes in v3:
time: 37.1 us; the launch traced here: 36.8 us
  Pallas kernels  33.9 us (91%)
  local copies, waits for them, and re-layouts  2.89 us (8%)
    pallas_call x1, Pallas kernels, body(): pl.pallas_call(functools.partial(kernel, views, rows_of), out_shape=jax.S...  33.9 us
    unnamed x1, local copies, waits for them, and re-layouts  2.89 us

profile of v3, /device:TPU:1, one launch (start us, length us, event | category | flops | bytes accessed | tf_op | source)
XLA Modules:
  0.0 36.8 jit_solution(13194303038707504277)
XLA Ops:
  0.0 33.9 %light_field_update.1 = f32[3,3,48,1024]{3,2,1,0:T(8,128)} custom-call(s32[1,2,3]{2,1,0:T(2,128)} %bitcast.1, bf16[3,3,48,1024]{3,2,1,0:T(8,128)(2,1)} %layers_hbm.1, bf16[1,48,1024]{2,1,0:T(8,128)(2,1)} %target_hbm.1), custom_call_target="tpu_custom_call" | custom-call | tf_op jit(solution)/shard_map/light_field_update/pallas_call | solution.py:516
  33.9 2.9 %copy.5 = f32[3,3,48,1024]{3,2,1,0:T(8,128)} copy(f32[3,3,48,1024]{3,2,1,0:T(8,128)} %light_field_update.1) | data formatting | bytes 3538944

commit v4 on v3

--- a/solution.py
+++ b/solution.py
@@ -118,6 +118,79 @@
     lax.fori_loop(0, views, fill, 0, unroll=4)
     recv_win[me, EDGE : EDGE + rows, :] = send_win[me]
 
+    def shift_copy(j):
+        partner = lax.rem(me + j, views)
+        return pltpu.make_async_remote_copy(
+            src_ref=shift_out, dst_ref=shift_in.at[me], send_sem=shift_send.at[j],
+            recv_sem=shift_recv.at[me], device_id=(partner, row), device_id_type=MESH,
+        )
+
+    def win_copy(j):
+        partner = lax.rem(me + j, views)
+        return pltpu.make_async_remote_copy(
+            src_ref=send_win.at[partner], dst_ref=recv_win.at[me, pl.ds(EDGE, rows)],
+            send_sem=win_send.at[j], recv_sem=win_recv.at[me],
+            device_id=(partner, row), device_id_type=MESH,
+        )
+
+    def up_copy(j):
+        partner = lax.rem(me + j, views)
+        return pltpu.make_async_remote_copy(
+            src_ref=send_win.at[partner, pl.ds(0, EDGE)],
+            dst_ref=recv_win.at[me, pl.ds(EDGE + rows, EDGE)],
+            send_sem=up_send.at[j], recv_sem=up_recv.at[me],
+            device_id=(partner, row - 1), device_id_type=MESH,
+        )
+
+    def down_copy(j):
+        partner = lax.rem(me + j, views)
+        return pltpu.make_async_remote_copy(
+            src_ref=send_win.at[partner, pl.ds(rows - EDGE, EDGE)],
+            dst_ref=recv_win.at[me, pl.ds(0, EDGE)],
+            send_sem=down_send.at[j], recv_sem=down_recv.at[me],
+            device_id=(partner, row + 1), device_id_type=MESH,
+        )
+
+    def layer_copy(up):
+        return pltpu.make_async_remote_copy(
+            src_ref=halo_out.at[0 if up else 1], dst_ref=halo_in.at[1 if up else 0],
+            send_sem=lh_send.at[0 if up else 1], recv_sem=lh_recv.at[1 if up else 0],
+            device_id=(me, row - 1 if up else row + 1), device_id_type=MESH,
+        )
+
+    def arrived(dst, sem):
+        return pltpu.make_async_remote_copy(
+            src_ref=dst, dst_ref=dst, send_sem=sem, recv_sem=sem,
+            device_id=(me, row), device_id_type=MESH,
+        ).wait_recv()
+
+    pl.semaphore_wait(
+        barrier, views - 1 + views * (above.astype(jnp.int32) + below.astype(jnp.int32))
+    )
+
+    def send_shift(j, carry):
+        shift_copy(j).start()
+        return carry
+
+    lax.fori_loop(1, views, send_shift, 0)
+
+    def send_all(j, carry):
+        @pl.when(j > 0)
+        def _():
+            win_copy(j).start()
+
+        @pl.when(above)
+        def _():
+            up_copy(j).start()
+
+        @pl.when(below)
+        def _():
+            down_copy(j).start()
+
+        return carry
+
+    lax.fori_loop(0, views, send_all, 0)
+
     fetch_layers.wait()
     for f in range(frames):
         for k in range(layer_count):
@@ -131,62 +204,6 @@
             halo_out[0, at] = plane[:EDGE].astype(jnp.bfloat16)
             halo_out[1, at] = plane[rows - EDGE :].astype(jnp.bfloat16)
 
-    def shift_copy(j):
-        partner = lax.rem(me + j, views)
-        return pltpu.make_async_remote_copy(
-            src_ref=shift_out, dst_ref=shift_in.at[me], send_sem=shift_send.at[j],
-            recv_sem=shift_recv.at[me], device_id=(partner, row), device_id_type=MESH,
-        )
-
-    def win_copy(j):
-        partner = lax.rem(me + j, views)
-        return pltpu.make_async_remote_copy(
-            src_ref=send_win.at[partner], dst_ref=recv_win.at[me, pl.ds(EDGE, rows)],
-            send_sem=win_send.at[j], recv_sem=win_recv.at[me],
-            device_id=(partner, row), device_id_type=MESH,
-        )
-
-    def up_copy(j):
-        partner = lax.rem(me + j, views)
-        return pltpu.make_async_remote_copy(
-            src_ref=send_win.at[partner, pl.ds(0, EDGE)],
-            dst_ref=recv_win.at[me, pl.ds(EDGE + rows, EDGE)],
-            send_sem=up_send.at[j], recv_sem=up_recv.at[me],
-            device_id=(partner, row - 1), device_id_type=MESH,
-        )
-
-    def down_copy(j):
-        partner = lax.rem(me + j, views)
-        return pltpu.make_async_remote_copy(
-            src_ref=send_win.at[partner, pl.ds(rows - EDGE, EDGE)],
-            dst_ref=recv_win.at[me, pl.ds(0, EDGE)],
-            send_sem=down_send.at[j], recv_sem=down_recv.at[me],
-            device_id=(partner, row + 1), device_id_type=MESH,
-        )
-
-    def layer_copy(up):
-        return pltpu.make_async_remote_copy(
-            src_ref=halo_out.at[0 if up else 1], dst_ref=halo_in.at[1 if up else 0],
-            send_sem=lh_send.at[0 if up else 1], recv_sem=lh_recv.at[1 if up else 0],
-            device_id=(me, row - 1 if up else row + 1), device_id_type=MESH,
-        )
-
-    def arrived(dst, sem):
-        return pltpu.make_async_remote_copy(
-            src_ref=dst, dst_ref=dst, send_sem=sem, recv_sem=sem,
-            device_id=(me, row), device_id_type=MESH,
-        ).wait_recv()
-
-    pl.semaphore_wait(
-        barrier, views - 1 + views * (above.astype(jnp.int32) + below.astype(jnp.int32))
-    )
-
-    def send_shift(j, carry):
-        shift_copy(j).start()
-        return carry
-
-    lax.fori_loop(1, views, send_shift, 0)
-
     @pl.when(above)
     def _():
         layer_copy(True).start()
@@ -194,23 +211,6 @@
     @pl.when(below)
     def _():
         layer_copy(False).start()
-
-    def send_all(j, carry):
-        @pl.when(j > 0)
-        def _():
-            win_copy(j).start()
-
-        @pl.when(above)
-        def _():
-            up_copy(j).start()
-
-        @pl.when(below)
-        def _():
-            down_copy(j).start()
-
-        return carry
-
-    lax.fori_loop(0, views, send_all, 0)
 
     @pl.when(jnp.logical_not(above))
     def _():
@@ -415,25 +415,22 @@
                 arrived(slots.at[slot], slot_recv.at[slot])
 
         where = pl.ds(pl.multiple_of(tile * LANES, LANES), LANES)
-        parts = []
-        for i in range(per_tile):
-            code = slots[tile * per_tile + i].astype(jnp.int32).astype(jnp.float32)
-            parts.append(jnp.exp(code * step + middle))
+        parts = [slots[tile * per_tile + i].astype(jnp.int32) for i in range(per_tile)]
         for f in range(frames):
             for k in range(layer_count):
                 at = f * layer_count + k
+                spans = []
                 for g in range(groups):
-                    ratio = None
+                    code = None
                     for i in range(per_tile):
                         part = parts[i][at * short : (at + 1) * short]
                         turn = (strip * (i - g)) % LANES
                         if turn:
                             part = pltpu.roll(part, turn, 1)
-                        ratio = part if ratio is None else jnp.where(lane < strip * i, ratio, part)
-                    span = slice(g * short, (g + 1) * short)
-                    out_ref[f, k, span, where] = (
-                        layers_ref[f, k, span, where].astype(jnp.float32) * ratio
-                    )
+                        code = part if code is None else jnp.where(lane < strip * i, code, part)
+                    spans.append(code)
+                whole = jnp.concatenate(spans, axis=0) if groups > 1 else spans[0]
+                out_ref[f, k, :, where] = whole.astype(jnp.int16)
         store_tile(tile).start()
 
     early = strip == 64
@@ -513,9 +510,9 @@
     height, inner = rows + 2 * EDGE, rows + 2 * HALO
     dma = pltpu.SemaphoreType.DMA
     f32, bf16 = jnp.float32, jnp.bfloat16
-    return pl.pallas_call(
+    codes = pl.pallas_call(
         functools.partial(kernel, views, rows_of),
-        out_shape=jax.ShapeDtypeStruct(layers.shape, f32),
+        out_shape=jax.ShapeDtypeStruct(layers.shape, jnp.int16),
         in_specs=[
             pl.BlockSpec(memory_space=pltpu.HBM),
             pl.BlockSpec(memory_space=pltpu.HBM),
@@ -526,7 +523,7 @@
             pltpu.SMEM((1, 2, layer_count), jnp.int32),
             pltpu.VMEM(layers.shape, bf16),
             pltpu.VMEM(target.shape, bf16),
-            pltpu.VMEM(layers.shape, f32),
+            pltpu.VMEM(layers.shape, jnp.int16),
             dma((3,)),
             dma((cols // LANES,)),
             pltpu.VMEM((views, rows, LANES), bf16),
@@ -554,6 +551,8 @@
         ),
         name="light_field_update",
     )(jnp.swapaxes(shifts, 1, 2), layers, target)
+    middle, step = code_range(views)
+    return layers.astype(f32) * jnp.exp(codes.astype(f32) * step + middle)
 
 
 def solution(mesh):

time: 37.1 us -> 37.1 us (level)
  other arithmetic: 0 us -> 2.95 us
  local copies, waits for them, and re-layouts: 2.89 us -> 0.01 us
    mul x0 -> x1, other arithmetic: none -> 2.95 us  [body(): return layers.astype(f32) * jnp.exp(codes.astype(f32) * step + middle)]
    unnamed x1 -> x2, local copies, waits for them, and re-layouts: 2.89 us -> 0.01 us
where the time goes in v4:
time: 37.1 us; the launch traced here: 36.7 us
  Pallas kernels  33.7 us (91%)
  other arithmetic  2.95 us (8%)
    pallas_call x1, Pallas kernels, body(): pl.pallas_call(functools.partial(kernel, views, rows_of), out_shape=jax.S...  33.7 us
    mul x1, other arithmetic, body(): return layers.astype(f32) * jnp.exp(codes.astype(f32) * step + middle)  2.95 us

profile of v4, /device:TPU:1, one launch (start us, length us, event | category | flops | bytes accessed | tf_op | source)
XLA Modules:
  0.0 36.7 jit_solution(2449329587109756512)
XLA Ops:
  0.0 0.0 copy-start
  0.0 33.7 %light_field_update.1 = s16[3,3,48,1024]{3,2,1,0:T(8,128)(2,1)} custom-call(s32[1,2,3]{2,1,0:T(2,128)} %bitcast.1, bf16[3,3,48,1024]{3,2,1,0:T(8,128)(2,1)} %layers_hbm.1, bf16[1,48,1024]{2,1,0:T(8,128)(2,1)} %target_hbm.1), custom_call_target="tpu_custom_call" | custom-call | tf_op jit(solution)/shard_map/light_field_update/pallas_call | solution.py:513
  33.7 0.0 copy-done
  33.7 3.0 %exponential_multiply_fusion = f32[3,3,48,1024]{3,2,1,0:T(8,128)} fusion(s16[3,3,48,1024]{3,2,1,0:T(8,128)(2,1)} %light_field_update.1, bf16[3,3,48,1024]{3,2,1,0:T(8,128)(2,1)S(1)} %copy-done), kind=kLoop, calls=%fused_computation | loop fusion | flops 2211840 | bytes 3538944 | tf_op jit(solution)/shard_map/mul | solution.py:555
Async XLA Ops:
  0.0 33.7 %copy-start = (bf16[3,3,48,1024]{3,2,1,0:T(8,128)(2,1)S(1)}, bf16[3,3,48,1024]{3,2,1,0:T(8,128)(2,1)}, u32[]{:S(2)}) copy-start(bf16[3,3,48,1024]{3,2,1,0:T(8,128)(2,1)} %layers_hbm.1) | copy-start | bytes 2654212

commit v5 on v4

--- a/solution.py
+++ b/solution.py
@@ -13,6 +13,7 @@
 EDGE = 16
 MARGIN = 32
 REGULAR = 0.05
+BATCH = 2
 MESH = pl.DeviceIdType.MESH
 
 
@@ -250,60 +251,73 @@
 
     to_smem.wait()
 
-    def one_view(j, carry):
-        view = lax.rem(me + views - j, views)
-
-        @pl.when(j > 0)
-        def _():
-            arrived(recv_win.at[view, pl.ds(EDGE, rows)], win_recv.at[view])
-
-        @pl.when(above)
-        def _():
-            arrived(recv_win.at[view, pl.ds(0, EDGE)], down_recv.at[view])
-
-        @pl.when(below)
-        def _():
-            arrived(recv_win.at[view, pl.ds(EDGE + rows, EDGE)], up_recv.at[view])
-
-        target_win[...] = recv_win[view].astype(jnp.float32)
-        row_shift = [shift_smem[view, 0, 2 * k] for k in range(layer_count)]
-        col_shift = [shift_smem[view, 0, 2 * k + 1] for k in range(layer_count)]
-        there = [lax.rem(LANES - c, LANES) for c in col_shift]
-        back = [lax.rem(LANES + c, LANES) for c in col_shift]
-
-        total = None
-        for f in range(frames):
-            seen = [
-                pltpu.roll(
-                    layer_win[f * layer_count + k, pl.ds(EDGE - HALO + row_shift[k], inner), :],
-                    there[k], 1,
-                )
-                for k in range(layer_count)
-            ]
-            for k in range(layer_count):
-                rest = None
-                for i in range(layer_count):
-                    if i != k:
-                        rest = seen[i] if rest is None else rest * seen[i]
-                others_win[f * layer_count + k] = rest
-                if k == layer_count - 1:
-                    whole = rest * seen[k]
-                    total = whole if total is None else total + whole
-        shown_win[...] = total * third_win[...]
+    def some_views(n, carry):
+        views_now = []
+        for b in range(BATCH):
+            j = n * BATCH + b
+            view = lax.rem(me + views - j, views)
+            views_now.append(view)
+
+            @pl.when(j > 0)
+            def _():
+                arrived(recv_win.at[view, pl.ds(EDGE, rows)], win_recv.at[view])
+
+            @pl.when(above)
+            def _():
+                arrived(recv_win.at[view, pl.ds(0, EDGE)], down_recv.at[view])
+
+            @pl.when(below)
+            def _():
+                arrived(recv_win.at[view, pl.ds(EDGE + rows, EDGE)], up_recv.at[view])
+
+        row_shift, back = [], []
+        for b, view in enumerate(views_now):
+            target_win[b] = recv_win[view].astype(jnp.float32)
+            row_now = [shift_smem[view, 0, 2 * k] for k in range(layer_count)]
+            col_now = [shift_smem[view, 0, 2 * k + 1] for k in range(layer_count)]
+            there = [lax.rem(LANES - c, LANES) for c in col_now]
+            row_shift.append(row_now)
+            back.append([lax.rem(LANES + c, LANES) for c in col_now])
+            total = None
+            for f in range(frames):
+                seen = [
+                    pltpu.roll(
+                        layer_win[f * layer_count + k, pl.ds(EDGE - HALO + row_now[k], inner), :],
+                        there[k], 1,
+                    )
+                    for k in range(layer_count)
+                ]
+                for k in range(layer_count):
+                    rest = None
+                    for i in range(layer_count):
+                        if i != k:
+                            rest = seen[i] if rest is None else rest * seen[i]
+                    others_win[b, f * layer_count + k] = rest
+                    if k == layer_count - 1:
+                        whole = rest * seen[k]
+                        total = whole if total is None else total + whole
+            shown_win[b] = total * third_win[...]
 
         for k in range(layer_count):
-            image = pltpu.roll(target_win[pl.ds(EDGE - row_shift[k], rows), :], back[k], 1)
-            model = pltpu.roll(shown_win[pl.ds(HALO - row_shift[k], rows), :], back[k], 1)
+            image, model = [], []
+            for b in range(BATCH):
+                turn, by = back[b][k], row_shift[b][k]
+                image.append(pltpu.roll(target_win[b, pl.ds(EDGE - by, rows), :], turn, 1))
+                model.append(pltpu.roll(shown_win[b, pl.ds(HALO - by, rows), :], turn, 1))
             for f in range(frames):
                 at = f * layer_count + k
-                rest = pltpu.roll(
-                    others_win[at, pl.ds(HALO - row_shift[k], rows), :], back[k], 1
-                )
-                upper[at] += image * rest
-                lower[at] += model * rest
-        return carry
-
-    lax.fori_loop(0, views, one_view, 0)
+                up, low = upper[at], lower[at]
+                for b in range(BATCH):
+                    rest = pltpu.roll(
+                        others_win[b, at, pl.ds(HALO - row_shift[b][k], rows), :], back[b][k], 1
+                    )
+                    up += image[b] * rest
+                    low += model[b] * rest
+                upper[at] = up
+                lower[at] = low
+        return carry
+
+    lax.fori_loop(0, views // BATCH, some_views, 0)
 
     spare = packed.shape[0] - planes * short
     if spare:
@@ -534,9 +548,9 @@
             pltpu.VMEM((2, planes, EDGE, LANES), bf16),
             pltpu.VMEM((2, planes, EDGE, LANES), bf16),
             pltpu.VMEM((planes, height, LANES), f32),
-            pltpu.VMEM((height, LANES), f32),
-            pltpu.VMEM((planes, inner, LANES), f32),
-            pltpu.VMEM((inner, LANES), f32),
+            pltpu.VMEM((BATCH, height, LANES), f32),
+            pltpu.VMEM((BATCH, planes, inner, LANES), f32),
+            pltpu.VMEM((BATCH, inner, LANES), f32),
             pltpu.VMEM((inner, LANES), f32),
             pltpu.VMEM((planes, rows, LANES), f32),
             pltpu.VMEM((planes, rows, LANES), f32),

time: 37.1 us -> 36 us (0.970)
  the two profiles are of different devices: /device:TPU:1 before, /device:TPU:17 now
where the time goes in v5:
time: 36 us; the launch traced here: 35.8 us
  Pallas kernels  32.8 us (91%)
  other arithmetic  2.95 us (8%)
    pallas_call x1, Pallas kernels, body(): pl.pallas_call(functools.partial(kernel, views, rows_of), out_shape=jax.S...  32.8 us
    mul x1, other arithmetic, body(): return layers.astype(f32) * jnp.exp(codes.astype(f32) * step + middle)  2.95 us

profile of v5, /device:TPU:17, one launch (start us, length us, event | category | flops | bytes accessed | tf_op | source)
XLA Modules:
  0.0 35.8 jit_solution(10893042448036261359)
XLA Ops:
  0.0 0.0 copy-start
  0.0 32.8 %light_field_update.1 = s16[3,3,48,1024]{3,2,1,0:T(8,128)(2,1)} custom-call(s32[1,2,3]{2,1,0:T(2,128)} %bitcast.1, bf16[3,3,48,1024]{3,2,1,0:T(8,128)(2,1)} %layers_hbm.1, bf16[1,48,1024]{2,1,0:T(8,128)(2,1)} %target_hbm.1), custom_call_target="tpu_custom_call" | custom-call | tf_op jit(solution)/shard_map/light_field_update/pallas_call | solution.py:527
  32.8 0.0 copy-done
  32.9 3.0 %exponential_multiply_fusion = f32[3,3,48,1024]{3,2,1,0:T(8,128)} fusion(s16[3,3,48,1024]{3,2,1,0:T(8,128)(2,1)} %light_field_update.1, bf16[3,3,48,1024]{3,2,1,0:T(8,128)(2,1)S(1)} %copy-done), kind=kLoop, calls=%fused_computation | loop fusion | flops 2211840 | bytes 3538944 | tf_op jit(solution)/shard_map/mul | solution.py:569
Async XLA Ops:
  0.0 32.8 %copy-start = (bf16[3,3,48,1024]{3,2,1,0:T(8,128)(2,1)S(1)}, bf16[3,3,48,1024]{3,2,1,0:T(8,128)(2,1)}, u32[]{:S(2)}) copy-start(bf16[3,3,48,1024]{3,2,1,0:T(8,128)(2,1)} %layers_hbm.1) | copy-start | bytes 2654212

commit v6 on v5

--- a/solution.py
+++ b/solution.py
@@ -13,7 +13,7 @@
 EDGE = 16
 MARGIN = 32
 REGULAR = 0.05
-BATCH = 2
+BATCH = 4
 MESH = pl.DeviceIdType.MESH
 
 
@@ -98,8 +98,8 @@
         return jnp.where((col >= 0) & (col < cols), both, 0.0)
 
     fetch_shifts.wait()
-    place = lax.broadcasted_iota(jnp.int32, (8, LANES), 1)
-    block = jnp.zeros((8, LANES), jnp.int32)
+    place = lax.broadcasted_iota(jnp.int32, (1, LANES), 1)
+    block = jnp.zeros((1, LANES), jnp.int32)
     for k in range(layer_count):
         for axis in range(2):
             block = jnp.where(place == 2 * k + axis, shifts_ref[0, axis, k], block)
@@ -407,6 +407,33 @@
 
             visit(d, act)
     spread(0)
+
+    @pl.when(above)
+    def _():
+        layer_copy(True).wait_send()
+
+    @pl.when(below)
+    def _():
+        layer_copy(False).wait_send()
+
+    def finish(j, carry):
+        @pl.when(j > 0)
+        def _():
+            shift_copy(j).wait_send()
+            win_copy(j).wait_send()
+
+        @pl.when(above)
+        def _():
+            up_copy(j).wait_send()
+
+        @pl.when(below)
+        def _():
+            down_copy(j).wait_send()
+
+        return carry
+
+    lax.fori_loop(0, views, finish, 0)
+
     for distance in range(1, depth):
         for d in both_ways(distance):
             column_step(d)
@@ -480,32 +507,6 @@
                     to_core(d, dx).wait_send()
 
             visit(d, act)
-
-    @pl.when(above)
-    def _():
-        layer_copy(True).wait_send()
-
-    @pl.when(below)
-    def _():
-        layer_copy(False).wait_send()
-
-    def finish(j, carry):
-        @pl.when(j > 0)
-        def _():
-            shift_copy(j).wait_send()
-            win_copy(j).wait_send()
-
-        @pl.when(above)
-        def _():
-            up_copy(j).wait_send()
-
-        @pl.when(below)
-        def _():
-            down_copy(j).wait_send()
-
-        return carry
-
-    lax.fori_loop(0, views, finish, 0)
 
     def wait_store(tile, carry):
         store_tile(tile).wait()
@@ -542,9 +543,9 @@
             dma((cols // LANES,)),
             pltpu.VMEM((views, rows, LANES), bf16),
             pltpu.VMEM((views, height, LANES), bf16),
-            pltpu.VMEM((8, LANES), jnp.int32),
-            pltpu.VMEM((views, 8, LANES), jnp.int32),
-            pltpu.SMEM((views, 8, LANES), jnp.int32),
+            pltpu.VMEM((1, LANES), jnp.int32),
+            pltpu.VMEM((views, 1, LANES), jnp.int32),
+            pltpu.SMEM((views, 1, LANES), jnp.int32),
             pltpu.VMEM((2, planes, EDGE, LANES), bf16),
             pltpu.VMEM((2, planes, EDGE, LANES), bf16),
             pltpu.VMEM((planes, height, LANES), f32),

time: 36 us -> 34.1 us (0.947)
  the two profiles are of different devices: /device:TPU:17 before, /device:TPU:1 now
where the time goes in v6:
time: 34.1 us; the launch traced here: 33.9 us
  Pallas kernels  30.9 us (91%)
  other arithmetic  2.95 us (9%)
    pallas_call x1, Pallas kernels, body(): pl.pallas_call(functools.partial(kernel, views, rows_of), out_shape=jax.S...  30.9 us
    mul x1, other arithmetic, body(): return layers.astype(f32) * jnp.exp(codes.astype(f32) * step + middle)  2.95 us

profile of v6, /device:TPU:1, one launch (start us, length us, event | category | flops | bytes accessed | tf_op | source)
XLA Modules:
  0.0 33.9 jit_solution(12739928082620777112)
XLA Ops:
  0.0 0.0 copy-start
  0.0 30.9 %light_field_update.1 = s16[3,3,48,1024]{3,2,1,0:T(8,128)(2,1)} custom-call(s32[1,2,3]{2,1,0:T(2,128)} %bitcast.1, bf16[3,3,48,1024]{3,2,1,0:T(8,128)(2,1)} %layers_hbm.1, bf16[1,48,1024]{2,1,0:T(8,128)(2,1)} %target_hbm.1), custom_call_target="tpu_custom_call" | custom-call | tf_op jit(solution)/shard_map/light_field_update/pallas_call | solution.py:528
  30.9 0.0 copy-done
  31.0 3.0 %exponential_multiply_fusion = f32[3,3,48,1024]{3,2,1,0:T(8,128)} fusion(s16[3,3,48,1024]{3,2,1,0:T(8,128)(2,1)} %light_field_update.1, bf16[3,3,48,1024]{3,2,1,0:T(8,128)(2,1)S(1)} %copy-done), kind=kLoop, calls=%fused_computation | loop fusion | flops 2211840 | bytes 3538944 | tf_op jit(solution)/shard_map/mul | solution.py:570
Async XLA Ops:
  0.0 30.9 %copy-start = (bf16[3,3,48,1024]{3,2,1,0:T(8,128)(2,1)S(1)}, bf16[3,3,48,1024]{3,2,1,0:T(8,128)(2,1)}, u32[]{:S(2)}) copy-start(bf16[3,3,48,1024]{3,2,1,0:T(8,128)(2,1)} %layers_hbm.1) | copy-start | bytes 2654212

commit v7 on v6

--- a/solution.py
+++ b/solution.py
@@ -80,7 +80,7 @@
 
         return carry
 
-    lax.fori_loop(0, views, greet, 0)
+    lax.fori_loop(0, views, greet, 0, unroll=4)
 
     lane = lax.broadcasted_iota(jnp.int32, (1, LANES), 1)
 
@@ -116,7 +116,7 @@
         send_win[c] = window(load, c).astype(jnp.bfloat16)
         return carry
 
-    lax.fori_loop(0, views, fill, 0, unroll=4)
+    lax.fori_loop(0, views, fill, 0, unroll=8)
     recv_win[me, EDGE : EDGE + rows, :] = send_win[me]
 
     def shift_copy(j):
@@ -513,6 +513,32 @@
         return carry
 
     lax.fori_loop(0, tiles, wait_store, 0)
+
+
+def decode(views, codes_hbm, layers_hbm, out_hbm, codes, layers, out, sems):
+    frames, layer_count = layers.shape[:2]
+    middle, step = code_range(views)
+    moves = []
+    for f in range(frames):
+        for k in range(layer_count):
+            at = f * layer_count + k
+            moves.append((
+                pltpu.make_async_copy(codes_hbm.at[f, k], codes.at[f, k], sems.at[0, at]),
+                pltpu.make_async_copy(layers_hbm.at[f, k], layers.at[f, k], sems.at[1, at]),
+                pltpu.make_async_copy(out.at[f, k], out_hbm.at[f, k], sems.at[2, at]),
+            ))
+    for code_in, layer_in, _ in moves:
+        code_in.start()
+        layer_in.start()
+    for at, (code_in, layer_in, store) in enumerate(moves):
+        f, k = at // layer_count, at % layer_count
+        code_in.wait()
+        layer_in.wait()
+        ratio = jnp.exp(codes[f, k].astype(jnp.int32).astype(jnp.float32) * step + middle)
+        out[f, k] = layers[f, k].astype(jnp.float32) * ratio
+        store.start()
+    for _, _, store in moves:
+        store.wait()
 
 
 def body(views, rows_of, layers, target, shifts):
@@ -566,8 +592,20 @@
         ),
         name="light_field_update",
     )(jnp.swapaxes(shifts, 1, 2), layers, target)
-    middle, step = code_range(views)
-    return layers.astype(f32) * jnp.exp(codes.astype(f32) * step + middle)
+    return pl.pallas_call(
+        functools.partial(decode, views),
+        out_shape=jax.ShapeDtypeStruct(layers.shape, f32),
+        in_specs=[pl.BlockSpec(memory_space=pltpu.HBM)] * 2,
+        out_specs=pl.BlockSpec(memory_space=pltpu.HBM),
+        scratch_shapes=[
+            pltpu.VMEM(layers.shape, jnp.int16),
+            pltpu.VMEM(layers.shape, bf16),
+            pltpu.VMEM(layers.shape, f32),
+            dma((3, planes)),
+        ],
+        compiler_params=pltpu.CompilerParams(vmem_limit_bytes=62 * 1024 * 1024),
+        name="decode_ratio",
+    )(codes, layers)
 
 
 def solution(mesh):

time: 34.1 us -> 33.6 us (0.985)
  other arithmetic: 2.95 us -> 0 us
  Pallas kernels: 30.9 us -> 33.4 us
    mul x1 -> x0, other arithmetic: 2.95 us -> none  [body(): return layers.astype(f32) * jnp.exp(codes.astype(f32) * step + middle)]
    pallas_call x0 -> x1, Pallas kernels: none -> 2.51 us  [body(): pl.pallas_call(functools.partial(decode, views), out_shape=jax.ShapeDtype...]
where the time goes in v7:
time: 33.6 us; the launch traced here: 33.5 us
  Pallas kernels  33.4 us (99%)
    pallas_call x1, Pallas kernels, body(): pl.pallas_call(functools.partial(kernel, views, rows_of), out_shape=jax.S...  30.9 us
    pallas_call x1, Pallas kernels, body(): pl.pallas_call(functools.partial(decode, views), out_shape=jax.ShapeDtype...  2.51 us

profile of v7, /device:TPU:1, one launch (start us, length us, event | category | flops | bytes accessed | tf_op | source)
XLA Modules:
  0.0 33.5 jit_solution(9632801346998516505)
XLA Ops:
  0.0 30.9 %light_field_update.1.codes_hbm = s16[3,3,48,1024]{3,2,1,0:T(8,128)(2,1)} custom-call(s32[1,2,3]{2,1,0:T(2,128)} %bitcast.1, bf16[3,3,48,1024]{3,2,1,0:T(8,128)(2,1)} %layers_hbm.3, bf16[1,48,1024]{2,1,0:T(8,128)(2,1)} %target_hbm.1), custom_call_target="tpu_custom_call" | custom-call | tf_op jit(solution)/shard_map/light_field_update/pallas_call | solution.py:554
  30.9 2.5 %decode_ratio.1 = f32[3,3,48,1024]{3,2,1,0:T(8,128)} custom-call(s16[3,3,48,1024]{3,2,1,0:T(8,128)(2,1)} %light_field_update.1.codes_hbm, bf16[3,3,48,1024]{3,2,1,0:T(8,128)(2,1)} %layers_hbm.3), custom_call_target="tpu_custom_call" | custom-call | tf_op jit(solution)/shard_map/decode_ratio/pallas_call | solution.py:595

commit v8 on v7

--- a/solution.py
+++ b/solution.py
@@ -319,18 +319,6 @@
 
     lax.fori_loop(0, views // BATCH, some_views, 0)
 
-    spare = packed.shape[0] - planes * short
-    if spare:
-        packed[planes * short :, :] = jnp.zeros((spare, LANES), jnp.float32)
-    for at in range(planes):
-        ratio = (upper[at] + REGULAR) / (lower[at] + REGULAR)
-        value = (jnp.log(ratio) - middle) * (1.0 / step)
-        merged = pltpu.roll(value[:short], LANES - MARGIN, 1)
-        if groups == 2:
-            merged = jnp.where(lane < strip, merged, pltpu.roll(value[short:], strip - MARGIN, 1))
-        packed[at * short : (at + 1) * short, :] = merged
-    slots[me] = jnp.round(packed[...]).astype(jnp.int32).astype(jnp.int16)
-
     core = lax.rem(me, 2)
     x = lax.rem(me // 2, across)
     z = me // (2 * across)
@@ -338,26 +326,34 @@
     def index(zz, xx, cc):
         return (zz * across + xx) * 2 + cc
 
-    def slot_copy(slot, to, sem):
+    chunks = 2 if packed.shape[0] % 32 == 0 else 1
+    size = packed.shape[0] // chunks
+
+    def part_of(slot, c):
+        return slots.at[slot, pl.ds(c * size, size)]
+
+    def slot_copy(slot, to, sem, c):
         return pltpu.make_async_remote_copy(
-            src_ref=slots.at[slot], dst_ref=slots.at[slot], send_sem=sem,
-            recv_sem=slot_recv.at[slot], device_id=(to, row), device_id_type=MESH,
+            src_ref=part_of(slot, c), dst_ref=part_of(slot, c), send_sem=sem,
+            recv_sem=slot_recv.at[c, slot], device_id=(to, row), device_id_type=MESH,
         )
+
+    def slot_here(slot, c):
+        arrived(part_of(slot, c), slot_recv.at[c, slot])
 
     def along(d):
         return index(z + d, x, core)
 
-    def to_column(d):
-        return slot_copy(me, index(z + d, x, core), col_send.at[depth + d])
-
-    def to_across(d, dx):
-        return slot_copy(
-            along(d), index(z, lax.rem(x + dx, across), core), x_send.at[depth + d, dx]
-        )
-
-    def to_core(d, dx):
+    def to_column(d, c):
+        return slot_copy(me, index(z + d, x, core), col_send.at[c, depth + d], c)
+
+    def to_across(d, dx, c):
+        to = index(z, lax.rem(x + dx, across), core)
+        return slot_copy(along(d), to, x_send.at[c, depth + d, dx], c)
+
+    def to_core(d, dx, c):
         slot = index(z + d, lax.rem(x + across - dx, across), core)
-        return slot_copy(slot, index(z, x, 1 - core), core_send.at[depth + d, dx])
+        return slot_copy(slot, index(z, x, 1 - core), core_send.at[c, depth + d, dx], c)
 
     def exists(d):
         return (z + d >= 0) & (z + d < depth)
@@ -371,42 +367,56 @@
     def both_ways(d):
         return (-d, d) if d else (0,)
 
-    def each_copy(d, act):
+    def each_copy(d, act, c):
         if d:
-            act(to_column(d))
+            act(to_column(d, c))
         for dx in range(1, across):
-            act(to_across(d, dx))
-        act(to_core(d, 0))
-
-    def spread(d):
+            act(to_across(d, dx, c))
+        act(to_core(d, 0, c))
+
+    def spread(d, c):
         for dx in range(1, across):
-            to_across(d, dx).start()
-        to_core(d, 0).start()
-
-    def column_step(d):
+            to_across(d, dx, c).start()
+        to_core(d, 0, c).start()
+
+    def column_step(d, c):
         def act():
-            slot = along(d)
-            arrived(slots.at[slot], slot_recv.at[slot])
-            spread(d)
+            slot_here(along(d), c)
+            spread(d, c)
 
         visit(d, act)
 
-    def across_step(d):
+    def across_step(d, c):
         def act():
             for dx in range(1, across):
-                slot = index(z + d, lax.rem(x + across - dx, across), core)
-                arrived(slots.at[slot], slot_recv.at[slot])
-                to_core(d, dx).start()
+                slot_here(index(z + d, lax.rem(x + across - dx, across), core), c)
+                to_core(d, dx, c).start()
 
         visit(d, act)
 
-    for distance in range(depth - 1, 0, -1):
-        for d in both_ways(distance):
-            def act():
-                to_column(d).start()
-
-            visit(d, act)
-    spread(0)
+    spare = packed.shape[0] - planes * short
+    if spare:
+        packed[planes * short :, :] = jnp.zeros((spare, LANES), jnp.float32)
+    done = 0
+    for c in range(chunks):
+        while done < planes and done * short < (c + 1) * size:
+            ratio = (upper[done] + REGULAR) / (lower[done] + REGULAR)
+            value = (jnp.log(ratio) - middle) * (1.0 / step)
+            merged = pltpu.roll(value[:short], LANES - MARGIN, 1)
+            if groups == 2:
+                other = pltpu.roll(value[short:], strip - MARGIN, 1)
+                merged = jnp.where(lane < strip, merged, other)
+            packed[done * short : (done + 1) * short, :] = merged
+            done += 1
+        span = slice(c * size, (c + 1) * size)
+        slots[me, span, :] = jnp.round(packed[span, :]).astype(jnp.int32).astype(jnp.int16)
+        for distance in range(depth - 1, 0, -1):
+            for d in both_ways(distance):
+                def act():
+                    to_column(d, c).start()
+
+                visit(d, act)
+        spread(0, c)
 
     @pl.when(above)
     def _():
@@ -435,10 +445,11 @@
     lax.fori_loop(0, views, finish, 0)
 
     for distance in range(1, depth):
-        for d in both_ways(distance):
-            column_step(d)
-        for d in both_ways(distance - 1):
-            across_step(d)
+        for c in range(chunks):
+            for d in both_ways(distance):
+                column_step(d, c)
+            for d in both_ways(distance - 1):
+                across_step(d, c)
 
     per_tile = LANES // strip
 
@@ -452,8 +463,8 @@
         for i in range(per_tile):
             @pl.when(lax.rem(tile * per_tile + i, 2) != core)
             def _():
-                slot = tile * per_tile + i
-                arrived(slots.at[slot], slot_recv.at[slot])
+                for c in range(chunks):
+                    slot_here(tile * per_tile + i, c)
 
         where = pl.ds(pl.multiple_of(tile * LANES, LANES), LANES)
         parts = [slots[tile * per_tile + i].astype(jnp.int32) for i in range(per_tile)]
@@ -482,8 +493,9 @@
 
     if early:
         lax.fori_loop(0, depth, unpack_column, 0)
-    for d in both_ways(depth - 1):
-        across_step(d)
+    for c in range(chunks):
+        for d in both_ways(depth - 1):
+            across_step(d, c)
 
     def unpack_rest(n, carry):
         zz, dx = n // (across - 1), lax.rem(n, across - 1) + 1
@@ -502,9 +514,10 @@
     for distance in range(depth):
         for d in both_ways(distance):
             def act():
-                each_copy(d, lambda copy: copy.wait_send())
-                for dx in range(1, across):
-                    to_core(d, dx).wait_send()
+                for c in range(chunks):
+                    each_copy(d, lambda copy: copy.wait_send(), c)
+                    for dx in range(1, across):
+                        to_core(d, dx, c).wait_send()
 
             visit(d, act)
 
@@ -585,7 +598,7 @@
             pltpu.VMEM((views, packed_rows, LANES), jnp.int16),
             dma((views,)), dma((views,)), dma((views,)), dma((views,)), dma((views,)), dma((views,)),
             dma((views,)), dma((views,)), dma, dma((2,)), dma((2,)),
-            dma((2 * depth,)), dma((2 * depth, across)), dma((2 * depth, across)), dma((views,)),
+            dma((2, 2 * depth)), dma((2, 2 * depth, across)), dma((2, 2 * depth, across)), dma((2, views)),
         ],
         compiler_params=pltpu.CompilerParams(
             collective_id=0, has_side_effects=True, vmem_limit_bytes=62 * 1024 * 1024

time: 33.6 us -> 32.9 us (0.979)
  Pallas kernels: 33.4 us -> 32.7 us
    pallas_call x1, Pallas kernels: 30.9 us -> 30.2 us  [body(): pl.pallas_call(functools.partial(kernel, views, rows_of), out_shape=jax.S...]
where the time goes in v8:
time: 32.9 us; the launch traced here: 32.7 us
  Pallas kernels  32.7 us (99%)
    pallas_call x1, Pallas kernels, body(): pl.pallas_call(functools.partial(kernel, views, rows_of), out_shape=jax.S...  30.2 us
    pallas_call x1, Pallas kernels, body(): pl.pallas_call(functools.partial(decode, views), out_shape=jax.ShapeDtype...  2.51 us

profile of v8, /device:TPU:1, one launch (start us, length us, event | category | flops | bytes accessed | tf_op | source)
XLA Modules:
  0.0 32.7 jit_solution(2615909772937251275)
XLA Ops:
  0.0 30.2 %light_field_update.1.codes_hbm = s16[3,3,48,1024]{3,2,1,0:T(8,128)(2,1)} custom-call(s32[1,2,3]{2,1,0:T(2,128)} %bitcast.1, bf16[3,3,48,1024]{3,2,1,0:T(8,128)(2,1)} %layers_hbm.3, bf16[1,48,1024]{2,1,0:T(8,128)(2,1)} %target_hbm.1), custom_call_target="tpu_custom_call" | custom-call | tf_op jit(solution)/shard_map/light_field_update/pallas_call | solution.py:567
  30.2 2.5 %decode_ratio.1 = f32[3,3,48,1024]{3,2,1,0:T(8,128)} custom-call(s16[3,3,48,1024]{3,2,1,0:T(8,128)(2,1)} %light_field_update.1.codes_hbm, bf16[3,3,48,1024]{3,2,1,0:T(8,128)(2,1)} %layers_hbm.3), custom_call_target="tpu_custom_call" | custom-call | tf_op jit(solution)/shard_map/decode_ratio/pallas_call | solution.py:608

commit v9 on v8

--- a/solution.py
+++ b/solution.py
@@ -410,13 +410,13 @@
             done += 1
         span = slice(c * size, (c + 1) * size)
         slots[me, span, :] = jnp.round(packed[span, :]).astype(jnp.int32).astype(jnp.int16)
-        for distance in range(depth - 1, 0, -1):
+        spread(0, c)
+        for distance in range(1, depth):
             for d in both_ways(distance):
                 def act():
                     to_column(d, c).start()
 
                 visit(d, act)
-        spread(0, c)
 
     @pl.when(above)
     def _():

time: 32.9 us -> 32.8 us (level)
  no operation moved by 1% of the time
where the time goes in v9:
time: 32.8 us; the launch traced here: 32.7 us
  Pallas kernels  32.7 us (100%)
    pallas_call x1, Pallas kernels, body(): pl.pallas_call(functools.partial(kernel, views, rows_of), out_shape=jax.S...  30.1 us
    pallas_call x1, Pallas kernels, body(): pl.pallas_call(functools.partial(decode, views), out_shape=jax.ShapeDtype...  2.51 us

profile of v9, /device:TPU:1, one launch (start us, length us, event | category | flops | bytes accessed | tf_op | source)
XLA Modules:
  0.0 32.7 jit_solution(7782420928812294154)
XLA Ops:
  0.0 30.1 %light_field_update.1.codes_hbm = s16[3,3,48,1024]{3,2,1,0:T(8,128)(2,1)} custom-call(s32[1,2,3]{2,1,0:T(2,128)} %bitcast.1, bf16[3,3,48,1024]{3,2,1,0:T(8,128)(2,1)} %layers_hbm.3, bf16[1,48,1024]{2,1,0:T(8,128)(2,1)} %target_hbm.1), custom_call_target="tpu_custom_call" | custom-call | tf_op jit(solution)/shard_map/light_field_update/pallas_call | solution.py:567
  30.2 2.5 %decode_ratio.1 = f32[3,3,48,1024]{3,2,1,0:T(8,128)} custom-call(s16[3,3,48,1024]{3,2,1,0:T(8,128)(2,1)} %light_field_update.1.codes_hbm, bf16[3,3,48,1024]{3,2,1,0:T(8,128)(2,1)} %layers_hbm.3), custom_call_target="tpu_custom_call" | custom-call | tf_op jit(solution)/shard_map/decode_ratio/pallas_call | solution.py:608

commit v10 on v9

--- a/solution.py
+++ b/solution.py
@@ -173,7 +173,7 @@
         shift_copy(j).start()
         return carry
 
-    lax.fori_loop(1, views, send_shift, 0)
+    lax.fori_loop(1, views, send_shift, 0, unroll=5)
 
     def send_all(j, carry):
         @pl.when(j > 0)
@@ -190,7 +190,7 @@
 
         return carry
 
-    lax.fori_loop(0, views, send_all, 0)
+    lax.fori_loop(0, views, send_all, 0, unroll=4)
 
     fetch_layers.wait()
     for f in range(frames):
@@ -235,7 +235,7 @@
         arrived(shift_in.at[source], shift_recv.at[source])
         return carry
 
-    lax.fori_loop(1, views, wait_shift, 0)
+    lax.fori_loop(1, views, wait_shift, 0, unroll=5)
     to_smem = pltpu.make_async_copy(shift_in, shift_smem, smem_sem)
     to_smem.start()
 

time: 32.8 us -> 32.9 us (level)
  no operation moved by 1% of the time
where the time goes in v10:
time: 32.9 us; the launch traced here: 32.7 us
  Pallas kernels  32.7 us (99%)
    pallas_call x1, Pallas kernels, body(): pl.pallas_call(functools.partial(kernel, views, rows_of), out_shape=jax.S...  30.2 us
    pallas_call x1, Pallas kernels, body(): pl.pallas_call(functools.partial(decode, views), out_shape=jax.ShapeDtype...  2.51 us

profile of v10, /device:TPU:1, one launch (start us, length us, event | category | flops | bytes accessed | tf_op | source)
XLA Modules:
  0.0 32.7 jit_solution(13273010201750949149)
XLA Ops:
  0.0 30.2 %light_field_update.1.codes_hbm = s16[3,3,48,1024]{3,2,1,0:T(8,128)(2,1)} custom-call(s32[1,2,3]{2,1,0:T(2,128)} %bitcast.1, bf16[3,3,48,1024]{3,2,1,0:T(8,128)(2,1)} %layers_hbm.3, bf16[1,48,1024]{2,1,0:T(8,128)(2,1)} %target_hbm.1), custom_call_target="tpu_custom_call" | custom-call | tf_op jit(solution)/shard_map/light_field_update/pallas_call | solution.py:567
  30.2 2.5 %decode_ratio.1 = f32[3,3,48,1024]{3,2,1,0:T(8,128)} custom-call(s16[3,3,48,1024]{3,2,1,0:T(8,128)(2,1)} %light_field_update.1.codes_hbm, bf16[3,3,48,1024]{3,2,1,0:T(8,128)(2,1)} %layers_hbm.3), custom_call_target="tpu_custom_call" | custom-call | tf_op jit(solution)/shard_map/decode_ratio/pallas_call | solution.py:608
